TPU v7x, 32 devices: a whole 2x2x4 slice. The times are simulated.
32 devices in a mesh: ctx: 8 (over y, x, core), head: 4 (over z).
Axes of the slice: x: 2, y: 2, z: 4, core: 2. Of those that a mesh axis runs over, the one named last changes fastest.
Arguments:
- x_in: bfloat16 [12288, 8192], P(('ctx', 'head')), may hold values from -6 to 6
- dt_raw: bfloat16 [12288, 128], P(('ctx', 'head')), may hold values from -3 to 3
- bc_in: bfloat16 [12288, 256], P(('ctx', 'head')), may hold values from -6 to 6
- z_in: bfloat16 [12288, 8192], P(('ctx', 'head')), may hold values from -6 to 6
- conv_x: float32 [4, 8192], P(None, 'head'), may hold values from -3 to 3
- bias_x: float32 [8192], P('head'), may hold values from -3 to 3
- conv_bc: float32 [4, 256], replicated, may hold values from -3 to 3
- bias_bc: float32 [256], replicated, may hold values from -3 to 3
- dt_bias: float32 [128], P('head'), may hold values from -0.5 to 0.5
- a_log: float32 [128], P('head'), may hold values from -16 to -2
- d_skip: float32 [128], P('head'), may hold values from 0.5 to 1.5
- norm_gain: float32 [8192], replicated, may hold values from 0.5 to 1.5
Outputs:
- mixed: bfloat16 [12288, 8192], P(('ctx', 'head'))
All inputs are finite; a program needn't handle non-finite values.
Results may differ from a plain program's by a relative error of at most 0.0015.
The roundings to bfloat16 on the way count: a program that leaves them out, or rounds other values in their place, can miss the bound.
Values may be sent and summed in bfloat16 or wider, within the bound.
A program may use at most 128 MiB of HBM per device.

v0:
```python
import jax
import jax.numpy as jnp
from jax import lax
from jax.sharding import PartitionSpec as P

BLOCK = 256


def from_behind(value, axis, by):
    count = lax.axis_size(axis)
    pairs = [(i, i + by) for i in range(count) if 0 <= i + by < count]
    return lax.ppermute(value, axis, pairs)


def entering(value, axis, combine, identity):
    count, place = (lax.axis_size(axis), lax.axis_index(axis))
    everything = jax.tree.map(lambda part: lax.all_gather(part, axis), value)
    start = jax.tree.map(
        lambda part, zero: jnp.broadcast_to(jnp.asarray(zero, part.dtype), part.shape),
        value,
        identity,
    )

    def step(k, before):
        reached = k < place
        new = combine(before, jax.tree.map(lambda part: part[k], everything))
        return jax.tree.map(lambda a, b: jnp.where(reached, a, b), new, before)

    return lax.fori_loop(0, count, step, start)


def causal_conv(values, rim_rows, taps, offset):
    padded = jnp.concatenate([rim_rows.astype(jnp.float32), values.astype(jnp.float32)], 0)
    summed = (
        offset[None, :]
        + taps[0] * padded[0:-3]
        + taps[1] * padded[1:-2]
        + taps[2] * padded[2:-1]
        + taps[3] * padded[3:]
    )
    return jax.nn.silu(summed).astype(jnp.bfloat16)


def per_device(
    x_in, dt_raw, bc_in, z_in, conv_x, bias_x, conv_bc, bias_bc, dt_bias, a_log, d_skip, norm_gain
):
    x_group, dt_group = (
        lax.all_to_all(x_in, "head", split_axis=1, concat_axis=0, tiled=True),
        lax.all_to_all(dt_raw, "head", split_axis=1, concat_axis=0, tiled=True),
    )
    bc_group = lax.all_gather(bc_in, "head", axis=0, tiled=True)
    tail_rows = jnp.concatenate([x_group[-3:], bc_group[-3:]], 1)
    rim_rows = from_behind(tail_rows, "ctx", 1)
    x_width = x_group.shape[1]
    x_conv = causal_conv(x_group, rim_rows[:, :x_width], conv_x, bias_x)
    bc_conv = causal_conv(bc_group, rim_rows[:, x_width:], conv_bc, bias_bc)
    state_size = bc_in.shape[1] // 2
    seg_rows = x_group.shape[0]
    head_count = dt_group.shape[1]
    head_width = x_width // head_count
    nblk = seg_rows // BLOCK
    x_blk = x_conv.reshape(nblk, BLOCK, head_count, head_width)
    b_blk = bc_conv[:, :state_size].reshape(nblk, BLOCK, state_size)
    c_blk = bc_conv[:, state_size:].reshape(nblk, BLOCK, state_size)
    step_size = jax.nn.softplus(dt_group.astype(jnp.float32) + dt_bias[None, :])
    log_decay = step_size * (-jnp.exp(a_log))[None, :]
    dt_blk = step_size.reshape(nblk, BLOCK, head_count)
    cum_sum = jnp.cumsum(log_decay.reshape(nblk, BLOCK, head_count), axis=1)
    scores = jnp.einsum("ctn,csn->cts", c_blk, b_blk, preferred_element_type=jnp.float32)
    cum_t = cum_sum.transpose(0, 2, 1)
    lower = jnp.arange(BLOCK)[:, None] >= jnp.arange(BLOCK)[None, :]
    spread = jnp.exp(
        jnp.where(lower[None, None], cum_t[:, :, :, None] - cum_t[:, :, None, :], -1e30)
    )
    m_mat = (scores[:, None] * spread * dt_blk.transpose(0, 2, 1)[:, :, None, :]).astype(
        jnp.bfloat16
    )
    y_diag = jnp.einsum("chts,cshp->cthp", m_mat, x_blk, preferred_element_type=jnp.float32)
    weight = jnp.exp(cum_sum[:, -1:, :] - cum_sum) * dt_blk
    b_weighted = (b_blk.astype(jnp.float32)[:, :, None, :] * weight[:, :, :, None]).astype(
        jnp.bfloat16
    )
    st_new = jnp.einsum("cqhn,cqhp->chnp", b_weighted, x_blk, preferred_element_type=jnp.float32)
    totals = cum_sum[:, -1, :]
    local_states = [jnp.zeros((head_count, state_size, head_width), jnp.float32)]
    for blk_i in range(nblk):
        local_states.append(
            local_states[-1] * jnp.exp(totals[blk_i])[:, None, None] + st_new[blk_i]
        )
    summary = local_states[nblk]
    seg_decay = jnp.sum(totals, axis=0)

    def combine_pair(earlier, later):
        return (earlier[0] + later[0], earlier[1] * jnp.exp(later[0])[:, None, None] + later[1])

    identity = (jnp.zeros_like(seg_decay), jnp.zeros_like(summary))
    _, incoming = entering((seg_decay, summary), "ctx", combine_pair, identity)
    prior = jnp.cumsum(totals, axis=0) - totals
    h_in = incoming[None] * jnp.exp(prior)[:, :, None, None] + jnp.stack(local_states[:nblk], 0)
    h_bf = h_in.astype(jnp.bfloat16)
    y_off = (
        jnp.einsum("ctn,chnp->cthp", c_blk, h_bf, preferred_element_type=jnp.float32)
        * jnp.exp(cum_sum)[:, :, :, None]
    )
    y_out = (y_diag + y_off + d_skip[None, None, :, None] * x_blk.astype(jnp.float32)).astype(
        jnp.bfloat16
    )
    y_tokens = lax.all_to_all(
        y_out.reshape(seg_rows, x_width), "head", split_axis=0, concat_axis=1, tiled=True
    )
    gated = y_tokens.astype(jnp.float32) * jax.nn.silu(z_in.astype(jnp.float32))
    mean_sq = jnp.mean(gated * gated, axis=-1, keepdims=True)
    return (gated * lax.rsqrt(mean_sq + 1e-05) * norm_gain[None, :]).astype(jnp.bfloat16)


def solution(mesh):
    in_specs = (
        P(("ctx", "head"), None),
        P(("ctx", "head"), None),
        P(("ctx", "head"), None),
        P(("ctx", "head"), None),
        P(None, "head"),
        P("head"),
        P(),
        P(),
        P("head"),
        P("head"),
        P("head"),
        P(),
    )
    out_specs = P(("ctx", "head"), None)
    return jax.shard_map(
        per_device, mesh=mesh, in_specs=in_specs, out_specs=out_specs, check_vma=False
    )
```

profile of v0, /device:TPU:0, one launch (start us, length us, event | category | flops | bytes accessed | tf_op | source)
XLA Modules:
  0.0 576.8 jit_solution(8970700095015876307)
XLA Ops:
  6.5 1.6 copy.101
  8.2 6.3 %all-to-all-start.1 = ((bf16[384,4,32]{0,2,1:T(8,128)(2,1)}), bf16[384,4,32]{0,2,1:T(8,128)(2,1)S(1)}, u32[]{:S(2)}, u32[]{:S(2)}) async-start(bf16[384,4,32]{0,2,1:T(8,128)(2,1)} %bitcast.13), calls=%async_computation.1 | async-start | bytes 196608 | tf_op jit(solution)/shard_map/all_to_all | solution.py:49
  14.5 6.6 %copy.140 = bf16[48,4,8,2048]{3,2,0,1:T(8,128)(2,1)} copy(bf16[48,4,8,2048]{3,2,1,0:T(8,128)(2,1)} %bitcast.87) | data formatting | bytes 12582912 | tf_op jit(solution)/shard_map/all_to_all | solution.py:48
  21.1 5.4 all-to-all-start
  26.6 151.2 %all_gather.13 = bf16[1536,256]{1,0:T(8,128)(2,1)S(1)} all-gather(bf16[384,256]{1,0:T(8,128)(2,1)S(1)} %copy-done.4), channel_id=1, replica_groups=mesh['ctx'=8,'head'=4] {'head'}, dimensions={0}, use_global_device_ids=true | all-gather | bytes 983040 | tf_op jit(solution)/shard_map/all_gather | solution.py:51
  179.6 3.5 reduce-window.6
  187.8 4.2 bitcast_convert_fusion
  193.2 9.2 %multiply_convert_fusion.5 = bf16[1536,2048]{1,0:T(8,128)(2,1)} fusion(f32[1536,2048]{1,0:T(8,128)S(1)} %bitcast_convert_fusion, f32[3,2048]{1,0:T(4,128)S(1)} %slice_convert_fusion, f32[2048]{0:T(1024)S(1)} %bitcast.96, f32[2048]{0:T(1024)S(1)} %bitcast.97, f32[2048]{0:T(1024)S(1)} %bitcast.95, f32[2048]{0:T(1024)S(1)} %bitcast.94, f32[2048]{0:T(1024)S(1)} %copy-done.10), kind=kLoop, calls=%fused_computation.39 | loop fusion | flops 50331648 | bytes 18939904 | tf_op jit(solution)/shard_map/convert_element_type | solution.py:41
  202.4 18.6 %reshape.195 = bf16[6,256,32,64]{3,2,1,0:T(8,128)(2,1)} reshape(bf16[1536,2048]{1,0:T(8,128)(2,1)} %multiply_convert_fusion.5) | data formatting | bytes 12582912 | tf_op jit(solution)/shard_map/reshape | solution.py:62
  221.0 14.9 %copy.106 = bf16[6,256,32,64]{1,3,2,0:T(8,128)(2,1)} copy(bf16[6,256,32,64]{3,2,1,0:T(8,128)(2,1)} %reshape.195) | data formatting | bytes 12582912 | tf_op jit(solution)/shard_map/reshape | solution.py:62
  235.9 12.1 %fusion.20 = f32[6,32,128,64]{2,3,1,0:T(8,128)S(1)} fusion(bf16[6,256,32,64]{1,3,2,0:T(8,128)(2,1)} %copy.106, f32[6,256,32]{1,2,0:T(8,128)S(1)} %get-tuple-element.173, f32[6,256,128]{2,1,0:T(8,128)S(1)} %convert_element_type.76), kind=kOutput, calls=%fused_computation.29 | convolution fusion | flops 817889280 | bytes 13565952 | tf_op jit(solution)/shard_map/cqhn,cqhp->chnp/dot_general | solution.py:83
  248.0 2.7 copy-done.1
  250.7 1.8 slice_add_fusion
  254.8 14.4 %all-reduce = f32[256]{0:T(256)S(1)} all-reduce(f32[256]{0:T(256)S(1)} %dynamic-update-slice), channel_id=2, replica_groups=mesh['ctx'=8,'head'=4] {'ctx'}, use_global_device_ids=true, to_apply=%add | all-reduce | flops 256 | bytes 2048
  270.3 2.4 fusion.36
  273.8 1.5 fusion.51
  275.3 2.4 fusion.37
  277.7 31.5 %all-gather.3.cloned.1.call-done = f32[8,32,128,64]{2,3,1,0:T(8,128)} async-done(((f32[1,32,128,64]{2,3,1,0:T(8,128)}), f32[8,32,128,64]{2,3,1,0:T(8,128)}) %all-gather.3.cloned.1.call-update) | async-done | bytes 8388624 | tf_op jit(solution)/shard_map/all_gather | solution.py:17
  309.2 39.9 %while.14 = (s32[]{:T(128)}, f32[32,128,64]{2,1,0:T(8,128)}, s32[]{:T(128)}, f32[8,32]{1,0:T(8,128)S(1)}, f32[8,32,128,64]{2,3,1,0:T(8,128)}, /*index=5*/s32[]{:T(128)}, s32[]{:T(128)}) while((s32[]{:T(128)}, f32[32,128,64]{2,1,0:T(8,128)}, s32[]{:T(128)}, f32[8,32]{1,0:T(8,128)S(1)}, f32[8,32,128,64]{2,3,1,0:T(8,128)}, ...), condition=%wide.region_4.5_spmd.clone, body=%wide.region_3.4_spmd.clone.sunk | while | flops 1048580 | bytes 7340521 | solution.py:29
  309.2 1.3 constant_dynamic-slice_fusion.2
  311.1 1.7 fusion.60
  312.8 1.3 constant_dynamic-slice_fusion.2
  314.7 3.3 fusion.60
  318.0 1.3 constant_dynamic-slice_fusion.2
  319.9 3.3 fusion.60
  323.2 1.3 constant_dynamic-slice_fusion.2
  325.1 3.3 fusion.60
  328.4 1.3 constant_dynamic-slice_fusion.2
  330.3 3.3 fusion.60
  333.6 1.3 constant_dynamic-slice_fusion.2
  335.5 3.3 fusion.60
  338.7 1.3 constant_dynamic-slice_fusion.2
  340.7 3.3 fusion.60
  343.9 1.3 constant_dynamic-slice_fusion.2
  345.9 3.3 fusion.60
  349.1 2.2 copy.109
  351.3 3.7 add_convert_fusion
  355.1 1.8 fusion.52
  357.2 15.7 %fusion.23 = bf16[6,256,32,64]{1,3,2,0:T(8,128)(2,1)S(1)} fusion(bf16[6,256,32,64]{1,3,2,0:T(8,128)(2,1)S(1)} %bitcast.89, f32[6,256,32,64]{1,3,2,0:T(8,128)S(1)} %bitcast.85, f32[32]{0:T(128)S(1)} %copy-done.15, f32[6,256,32]{1,2,0:T(8,128)S(1)} %copy-done.6, f32[6,32,256]{2,1,0:T(8,128)S(1)} %copy-done.5, f32[6,32,256]{2,1,0:T(8,128)S(1)} %copy-done.3, ...), kind=kOutput, calls=%fused_computation.34 | convolution fusion | flops 1692401664 | bytes 27394176 | tf_op jit(solution)/shard_map/chts,cshp->cthp/dot_general | solution.py:78
  372.9 8.3 %copy.111 = bf16[6,256,32,64]{1,0,3,2:T(8,128)(2,1)} copy(bf16[6,256,32,64]{1,3,2,0:T(8,128)(2,1)S(1)} %fusion.23) | data formatting | bytes 12582912 | tf_op jit(solution)/shard_map/convert_element_type | solution.py:105
  381.3 13.8 %all_to_all.40 = bf16[4,384,2048]{1,0,2:T(4,128)(2,1)} reshape(bf16[6,256,32,64]{1,0,3,2:T(8,128)(2,1)} %copy.111) | data formatting | bytes 12582912 | tf_op jit(solution)/shard_map/all_to_all | solution.py:108
  395.1 6.2 %copy.112 = bf16[4,384,2048]{1,2,0:T(8,128)(2,1)} copy(bf16[4,384,2048]{1,0,2:T(4,128)(2,1)} %all_to_all.40) | data formatting | bytes 12582912 | tf_op jit(solution)/shard_map/all_to_all | solution.py:108
  401.3 5.2 all-to-all-start.2
  406.6 8.6 %copy.113 = bf16[384,8192]{0,1:T(8,128)(2,1)} copy(bf16[384,8192]{1,0:T(8,128)(2,1)} %param.17) | data formatting | bytes 12582912 | tf_op args[3]
  415.2 130.2 %all-to-all-done.2 = bf16[4,384,2048]{1,2,0:T(8,128)(2,1)} async-done(((bf16[4,384,2048]{1,2,0:T(8,128)(2,1)}), bf16[4,384,2048]{1,2,0:T(8,128)(2,1)}, u32[]{:S(2)}, u32[]{:S(2)}) %all-to-all-start.2) | async-done | bytes 6291488 | tf_op jit(solution)/shard_map/all_to_all | solution.py:108
  545.4 7.8 %multiply_reduce_fusion = f32[384]{0:T(512)S(1)} fusion(bf16[384,8192]{0,1:T(8,128)(2,1)} %copy.113, bf16[4,384,2048]{1,2,0:T(8,128)(2,1)} %all-to-all-done.2), kind=kLoop, calls=%fused_computation.36 | loop fusion | flops 28311168 | bytes 12584448 | tf_op jit(solution)/shard_map/reduce_sum | solution.py:112
  553.3 8.1 %multiply_convert_fusion.4 = bf16[384,8192]{0,1:T(8,128)(2,1)} fusion(f32[8192]{0:T(1024)S(1)} %copy-done.8, f32[384]{0:T(512)S(1)} %add_rsqrt_fusion, bf16[384,8192]{0,1:T(8,128)(2,1)S(1)} %copy-done, bf16[4,384,2048]{1,2,0:T(8,128)(2,1)} %all-to-all-done.2), kind=kLoop, calls=%fused_computation.35 | loop fusion | flops 31457280 | bytes 18908672 | tf_op jit(solution)/shard_map/convert_element_type | solution.py:113
  561.4 8.6 %copy.114 = bf16[384,8192]{1,0:T(8,128)(2,1)} copy(bf16[384,8192]{0,1:T(8,128)(2,1)} %multiply_convert_fusion.4) | data formatting | bytes 12582912 | tf_op jit(solution)/shard_map/convert_element_type | solution.py:113
  (95 shorter events, 16.6 us)
Async XLA Ops:
  8.2 12.9 %all-to-all-start.1 = ((bf16[384,4,32]{0,2,1:T(8,128)(2,1)}), bf16[384,4,32]{0,2,1:T(8,128)(2,1)S(1)}, u32[]{:S(2)}, u32[]{:S(2)}) async-start(bf16[384,4,32]{0,2,1:T(8,128)(2,1)} %bitcast.13), calls=%async_computation.1 | async-start | bytes 196608 | tf_op jit(solution)/shard_map/all_to_all | solution.py:49
  21.1 5.5 copy-start.4
  21.1 158.0 %copy-start.14 = (f32[32]{0:T(128)S(1)}, f32[32]{0:T(128)}, u32[]{:S(2)}) copy-start(f32[32]{0:T(128)} %param.23) | copy-start | bytes 388
  21.1 158.0 %copy-start.11 = (f32[4,256]{1,0:T(4,128)S(1)}, f32[4,256]{1,0:T(4,128)}, u32[]{:S(2)}) copy-start(f32[4,256]{1,0:T(4,128)} %param.20) | copy-start | bytes 12292
  21.1 158.0 %copy-start.9 = (f32[4,2048]{1,0:T(4,128)S(1)}, f32[4,2048]{1,0:T(4,128)}, u32[]{:S(2)}) copy-start(f32[4,2048]{1,0:T(4,128)} %param.18) | copy-start | bytes 98308
  21.1 158.3 %copy-start.12 = (f32[32]{0:T(128)S(1)}, f32[32]{0:T(128)}, u32[]{:S(2)}) copy-start(f32[32]{0:T(128)} %param.22) | copy-start | bytes 388
  21.1 164.5 %all-to-all-start = ((bf16[384,4,2048]{2,0,1:T(8,128)(2,1)}), bf16[384,4,2048]{2,0,1:T(8,128)(2,1)}, u32[]{:S(2)}, u32[]{:S(2)}) async-start(bf16[384,4,2048]{2,0,1:T(8,128)(2,1)} %bitcast.84), calls=%async_computation | async-start | bytes 12582912 | tf_op jit(solution)/shard_map/all_to_all | solution.py:48
  26.5 282.7 %all-gather.3.cloned.1.call-start = ((), (), s32[]{:S(2)}) async-start(), calls=%async_computation.3 | async-start | bytes 9437184 | tf_op jit(solution)/shard_map/all_gather | solution.py:17
  186.5 5.6 copy-start.13
  186.5 6.7 %copy-start.10 = (f32[2048]{0:T(1024)S(1)}, f32[2048]{0:T(1024)}, u32[]{:S(2)}) copy-start(f32[2048]{0:T(1024)} %param.19) | copy-start | bytes 24580
  186.5 5.6 collective-permute-start
  248.0 2.7 copy-start.1
  248.0 4.6 copy-start.16
  351.3 5.6 slice-start
  355.0 1.9 slice-start.1
  355.0 2.1 copy-start.2
  355.1 2.1 copy-start.3
  355.1 2.1 copy-start.5
  355.1 2.1 copy-start.6
  355.1 2.1 copy-start.7
  355.1 2.1 copy-start.15
  401.3 144.1 %all-to-all-start.2 = ((bf16[4,384,2048]{1,2,0:T(8,128)(2,1)}), bf16[4,384,2048]{1,2,0:T(8,128)(2,1)}, u32[]{:S(2)}, u32[]{:S(2)}) async-start(bf16[4,384,2048]{1,2,0:T(8,128)(2,1)} %copy.112), calls=%async_computation.2 | async-start | bytes 12582912 | tf_op jit(solution)/shard_map/all_to_all | solution.py:108
  415.2 138.1 %copy-start.8 = (f32[8192]{0:T(1024)S(1)}, f32[8192]{0:T(1024)}, u32[]{:S(2)}) copy-start(f32[8192]{0:T(1024)} %param.25) | copy-start | bytes 98308
  545.4 7.9 %copy-start = (bf16[384,8192]{0,1:T(8,128)(2,1)S(1)}, bf16[384,8192]{0,1:T(8,128)(2,1)}, u32[]{:S(2)}) copy-start(bf16[384,8192]{0,1:T(8,128)(2,1)} %copy.113) | copy-start | bytes 18874372
Sparse Core Ops, SparseCore 0:
  252.7 56.4 all-gather.2
where the time goes:
time: 580 us; the launch traced here: 577 us
  blocking collectives  166 us (29%)
  waiting for transfers between devices  162 us (28%)
  local copies, waits for them, and re-layouts  113 us (19%)
  other arithmetic  72 us (12%)
  matrix products  31.2 us (5%)
  starting transfers between devices  18.3 us (3%)
  between operations  14.5 us (2%)
    all_gather x1, blocking collectives, per_device(): bc_group = lax.all_gather(bc_in, 'head', axis=0, tiled=True)  151 us
    all_to_all x1, waiting for transfers between devices, per_device(): lax.all_to_all(y_out.reshape(seg_rows, x_width), 'head', split_axis=0, co...  130 us
    reshape x2, local copies, waits for them, and re-layouts, per_device(): x_blk = x_conv.reshape(nblk, BLOCK, head_count, head_width)  33.5 us
    all_gather x1, waiting for transfers between devices, entering(): everything = jax.tree.map(lambda part: lax.all_gather(part, axis), value)  31.5 us
    select_n x8, other arithmetic, step(): return jax.tree.map(lambda a, b: jnp.where(reached, a, b), new, before)  24.4 us
    all_to_all x2, local copies, waits for them, and re-layouts, per_device(): lax.all_to_all(y_out.reshape(seg_rows, x_width), 'head', split_axis=0, co...  20.1 us
    unnamed x46, local copies, waits for them, and re-layouts  17.3 us
    dot_general x1, matrix products, per_device(): jnp.einsum('chts,cshp->cthp', m_mat, x_blk, preferred_element_type=jnp.fl...  15.7 us
  transfers between devices with their start and end apart: 5, of which 2 were waited for; matrix products, arithmetic and copies ran while one was open for 6% of the time, Pallas kernels for 0%

commit v1 on v0

--- a/solution.py
+++ b/solution.py
@@ -1,6 +1,10 @@
+import functools
+
 import jax
 import jax.numpy as jnp
 from jax import lax
+from jax.experimental import pallas as pl
+from jax.experimental.pallas import tpu as pltpu
 from jax.sharding import PartitionSpec as P
 
 BLOCK = 256
@@ -41,7 +45,7 @@
     return jax.nn.silu(summed).astype(jnp.bfloat16)
 
 
-def per_device(
+def per_device_by_heads(
     x_in, dt_raw, bc_in, z_in, conv_x, bias_x, conv_bc, bias_bc, dt_bias, a_log, d_skip, norm_gain
 ):
     x_group, dt_group = (
@@ -113,6 +117,378 @@
     return (gated * lax.rsqrt(mean_sq + 1e-05) * norm_gain[None, :]).astype(jnp.bfloat16)
 
 
+HALF = 128
+RIM = 16
+STEP_HEADS = 8
+VMEM_BYTES = 56 * 1024 * 1024
+
+
+def silu(u):
+    return u / (1.0 + jnp.exp(-u))
+
+
+def rows_conv(halo, values, taps, offset):
+    rows, at = values.shape[0], halo.shape[0] - 3
+    padded = jnp.concatenate([halo.astype(jnp.float32), values.astype(jnp.float32)], 0)
+    summed = (
+        offset
+        + taps[0:1] * padded[at : at + rows]
+        + taps[1:2] * padded[at + 1 : at + 1 + rows]
+        + taps[2:3] * padded[at + 2 : at + 2 + rows]
+        + taps[3:4] * padded[at + 3 : at + 3 + rows]
+    )
+    return silu(summed).astype(jnp.bfloat16)
+
+
+def prep_kernel(
+    odd_ref, bc_ref, halo_ref, ebc_ref, taps_ref, bias_ref, dt_ref, edt_ref, dtb_ref, alog_ref,
+    c_ref, bt_ref, s_ref, g_ref, gt_ref, dtt_ref, wt_ref, ecs_ref, log_ref,
+):
+    odd = odd_ref[0] == 1
+    taps, bias = taps_ref[...], bias_ref[...]
+    ebc = ebc_ref[...].astype(jnp.float32)
+    bcc = jnp.concatenate(
+        [
+            rows_conv(ebc[:RIM], ebc[RIM:], taps, bias).astype(jnp.float32),
+            rows_conv(halo_ref[...], bc_ref[...], taps, bias).astype(jnp.float32),
+        ],
+        0,
+    ).astype(jnp.bfloat16)
+    n = bcc.shape[1] // 2
+    b, c = bcc[:, :n], bcc[:, n:]
+    c_ref[...] = c[HALF:]
+    bt_ref[...] = b.astype(jnp.float32).T.astype(jnp.bfloat16)
+
+    def score(i, j):
+        return lax.dot_general(
+            c[i * HALF : (i + 1) * HALF],
+            b[j * HALF : (j + 1) * HALF],
+            (((1,), (1,)), ((), ())),
+            preferred_element_type=jnp.float32,
+        )
+
+    for i in range(3):
+        s_ref[i] = score(i + 1, i + 1)
+    s_ref[3] = jnp.where(odd, score(3, 2), score(2, 1))
+    s_ref[4] = score(1, 0)
+
+    raw = [edt_ref[...].astype(jnp.float32)[RIM:], dt_ref[...].astype(jnp.float32)]
+    u = jnp.concatenate(raw, 0) + dtb_ref[...]
+    row = lax.broadcasted_iota(jnp.int32, u.shape, 0)
+    dt = jnp.maximum(u, 0.0) + jnp.log1p(jnp.exp(-jnp.abs(u)))
+    dt = jnp.where(jnp.logical_and(row < HALF, jnp.logical_not(odd)), 0.0, dt)
+    la = dt * (-jnp.exp(alog_ref[...]))
+    rows = la.shape[0]
+    at = lax.broadcasted_iota(jnp.int32, (rows, rows), 0)
+    of = lax.broadcasted_iota(jnp.int32, (rows, rows), 1)
+    g = jnp.dot(
+        (at >= of).astype(jnp.float32), la,
+        precision=lax.Precision.HIGHEST, preferred_element_type=jnp.float32,
+    )
+    cut = jnp.where(odd, 2 * HALF, 3 * HALF)
+    g_cut = jnp.where(odd, g[2 * HALF - 1 : 2 * HALF], g[3 * HALF - 1 : 3 * HALF])
+    g_end = g[rows - 1 : rows]
+    first = row < cut
+    ecs_ref[...] = jnp.exp(g - jnp.where(first, 0.0, g_cut))[HALF:]
+    weight = jnp.exp(jnp.where(first, g_cut, g_end) - g) * dt
+    g_ref[...] = g[HALF:]
+    gt_ref[...] = g.T
+    dtt_ref[...] = dt.T
+    wt_ref[...] = weight.T
+    log_ref[...] = jnp.concatenate(
+        [g_cut, g_end - g_cut, jnp.where(odd, g_end, g_cut), jnp.zeros((5, g.shape[1]))], 0
+    )
+
+
+def states_kernel(
+    odd_ref, x_ref, halo_ref, ex_ref, par_ref, bt_ref, wt_ref, dec_ref, xc_ref, st_ref, sum_ref
+):
+    odd = odd_ref[0] == 1
+    par = par_ref[...]
+    ex = ex_ref[...].astype(jnp.float32)
+    xc_ref[:HALF] = rows_conv(ex[:RIM], ex[RIM:], par[0:4], par[4:5])
+    xc_ref[HALF:] = rows_conv(halo_ref[...], x_ref[...], par[0:4], par[4:5])
+    bt = bt_ref[...].astype(jnp.float32)
+    wt = wt_ref[...]
+    n = bt.shape[0]
+    left = lax.broadcasted_iota(jnp.int32, (n, 128), 1) < 64
+    for pair in range(STEP_HEADS // 2):
+        lanes = slice(pair * 128, pair * 128 + 128)
+        parts = []
+        for i in range(4):
+            cols = slice(i * HALF, (i + 1) * HALF)
+            both = jnp.concatenate(
+                [
+                    (bt[:, cols] * wt[2 * pair + k : 2 * pair + k + 1, cols]).astype(jnp.bfloat16)
+                    for k in range(2)
+                ],
+                0,
+            )
+            full = jnp.dot(both, xc_ref[cols, lanes], preferred_element_type=jnp.float32)
+            parts.append(jnp.where(left, full[:n], full[n:]))
+        st_first = parts[1] + jnp.where(odd, parts[0], parts[2])
+        both_blocks = st_first * dec_ref[1:2, lanes] + (parts[2] + parts[3])
+        st_ref[0, :, lanes] = st_first
+        sum_ref[0, :, lanes] = jnp.where(odd, both_blocks, st_first)
+
+
+def diag_kernel(odd_ref, xc_ref, s_ref, g_ref, gt_ref, dtt_ref, par_ref, y_ref):
+    shift = odd_ref[0]
+    odd = shift == 1
+    g, gt, dtt = g_ref[0], gt_ref[...], dtt_ref[...]
+    t_at = lax.broadcasted_iota(jnp.int32, (HALF, HALF), 0)
+    s_at = lax.broadcasted_iota(jnp.int32, (HALF, HALF), 1)
+    lower = t_at >= s_at
+    left = s_at < 64
+    subs = [slice(i * HALF, (i + 1) * HALF) for i in range(3)]
+    g_off = jnp.where(odd, g[subs[2]], g[subs[1]])
+    behind = [slice(i * HALF, (i + 1) * HALF) for i in range(4)]
+    gt_off = jnp.where(odd, gt[:, behind[2]], gt[:, behind[1]])
+    dtt_off = jnp.where(odd, dtt[:, behind[2]], dtt[:, behind[1]])
+    x_off = xc_ref[pl.ds(pl.multiple_of(HALF + shift * HALF, HALF), HALF), :]
+    tiles = [(g[subs[i]], gt[:, at], dtt[:, at], xc_ref[at, :]) for i, at in enumerate(behind[1:])]
+    tiles.append((g_off, gt_off, dtt_off, x_off))
+    tiles.append((g[subs[0]], gt[:, behind[0]], dtt[:, behind[0]], xc_ref[behind[0], :]))
+    for pair in range(STEP_HEADS // 2):
+        lanes = slice(pair * 128, pair * 128 + 128)
+        results = []
+        for i, (g_t, g_s, dt_s, x_s) in enumerate(tiles):
+            both = []
+            for k in range(2):
+                h = 2 * pair + k
+                gap = g_t[:, h : h + 1] - g_s[h : h + 1]
+                if i < 3:
+                    gap = jnp.where(lower, gap, -1e30)
+                both.append(
+                    (s_ref[i] * jnp.exp(gap) * dt_s[h : h + 1]).astype(jnp.bfloat16)
+                )
+            full = jnp.dot(
+                jnp.concatenate(both, 0), x_s[:, lanes], preferred_element_type=jnp.float32
+            )
+            results.append(jnp.where(left, full[:HALF], full[HALF:]))
+        skip = par_ref[5:6, lanes]
+        for i in range(3):
+            y = results[i] + skip * tiles[i][3][:, lanes].astype(jnp.float32)
+            if i == 0:
+                y = y + results[4]
+            if i == 1:
+                y = y + jnp.where(odd, 0.0, results[3])
+            if i == 2:
+                y = y + jnp.where(odd, results[3], 0.0)
+            y_ref[subs[i], lanes] = y
+
+
+def gate_kernel(
+    odd_ref, y_ref, c_ref, ecs_ref, h_ref, st_ref, dec_ref, z_ref, gain_ref, out_ref, held
+):
+    early = pl.program_id(0) < 2 - odd_ref[0]
+    c = c_ref[...]
+    ecs = ecs_ref[...]
+    left = lax.broadcasted_iota(jnp.int32, (HALF, 128), 1) < 64
+    groups, _, width = h_ref.shape
+    wide = STEP_HEADS * 64
+    square = jnp.zeros((HALF, 128), jnp.float32)
+    for start in range(0, groups * width, wide):
+        group, off = divmod(start, width)
+        cols = slice(off, off + wide)
+        h = h_ref[group, :, cols]
+        later = h * dec_ref[0:1, start : start + wide] + st_ref[group, :, cols]
+        hb = jnp.where(early, h, later).astype(jnp.bfloat16)
+        far = jnp.dot(c, hb, preferred_element_type=jnp.float32)
+        for pair in range(STEP_HEADS // 2):
+            head = start // 64 + 2 * pair
+            lanes = slice(start + pair * 128, start + pair * 128 + 128)
+            scale = jnp.where(left, ecs[:, head : head + 1], ecs[:, head + 1 : head + 2])
+            y = y_ref[:, lanes] + far[:, pair * 128 : pair * 128 + 128] * scale
+            y = y.astype(jnp.bfloat16).astype(jnp.float32)
+            gated = y * silu(z_ref[:, lanes].astype(jnp.float32))
+            held[:, lanes] = gated
+            square = square + gated * gated
+    mean = jnp.sum(square, axis=1, keepdims=True) / (groups * width)
+    scale = lax.rsqrt(mean + 1e-5)
+    for start in range(0, groups * width, wide):
+        lanes = slice(start, start + wide)
+        out_ref[:, lanes] = (held[:, lanes] * scale * gain_ref[:, lanes]).astype(jnp.bfloat16)
+
+
+def params(**more):
+    return pltpu.CompilerParams(vmem_limit_bytes=VMEM_BYTES, **more)
+
+
+def per_device(
+    x_in, dt_raw, bc_in, z_in, conv_x, bias_x, conv_bc, bias_bc, dt_bias, a_log, d_skip, norm_gain
+):
+    f32, bf16 = jnp.float32, jnp.bfloat16
+    n_ctx, n_head = lax.axis_size("ctx"), lax.axis_size("head")
+    ctx, zed = lax.axis_index("ctx"), lax.axis_index("head")
+    rows, width = x_in.shape
+    heads = dt_raw.shape[1]
+    state = bc_in.shape[1] // 2
+    group_width = width // n_head
+    group_heads = heads // n_head
+    odd = (zed % 2).astype(jnp.int32).reshape(1)
+
+    small = jnp.concatenate([dt_bias, a_log, d_skip])
+    small = jnp.pad(small, (0, group_width - small.shape[0]))
+    mine = jnp.concatenate([conv_x, bias_x[None], small[None]], 0)
+    table = lax.all_gather(mine, "head")
+    par = jnp.concatenate([table[g] for g in range(n_head)], 1)
+    vectors = table[:, 5, : 3 * group_heads].reshape(n_head, 3, group_heads)
+    vectors = vectors.transpose(1, 0, 2).reshape(3, heads)
+    skip = jnp.repeat(vectors[2], width // heads)
+    par = jnp.concatenate([par[:5], skip[None], jnp.zeros((2, width), f32)], 0)
+    count = n_ctx * n_head
+    rim = jnp.concatenate([x_in[-RIM:], bc_in[-RIM:]], 1)
+    rim = lax.ppermute(rim, ("ctx", "head"), [(i, i + 1) for i in range(count - 1)])
+    halo_x, halo_bc = rim[:, :width], rim[:, width:]
+    last = rows - HALF - RIM
+    to_odd = [(i, i + 1) for i in range(0, n_head, 2)]
+    extra_x = lax.ppermute(x_in[last:], "head", to_odd)
+    extra_small = lax.ppermute(jnp.concatenate([bc_in[last:], dt_raw[last:]], 1), "head", to_odd)
+    extra_bc, extra_dt = extra_small[:, : 2 * state], extra_small[:, 2 * state :]
+    deep = rows + HALF
+
+    smem = pl.BlockSpec(memory_space=pltpu.SMEM)
+    vmem = pl.BlockSpec(memory_space=pltpu.VMEM)
+    shape = jax.ShapeDtypeStruct
+    c, bt, scores, g, gt, dtt, wt, ecs, logs = pl.pallas_call(
+        prep_kernel,
+        in_specs=[smem] + [vmem] * 9,
+        out_specs=[vmem] * 9,
+        out_shape=[
+            shape((rows, state), bf16),
+            shape((state, deep), bf16),
+            shape((5, HALF, HALF), f32),
+            shape((rows, heads), f32),
+            shape((heads, deep), f32),
+            shape((heads, deep), f32),
+            shape((heads, deep), f32),
+            shape((rows, heads), f32),
+            shape((8, heads), f32),
+        ],
+        compiler_params=params(),
+        name="prep",
+    )(
+        odd, bc_in, halo_bc, extra_bc, conv_bc, bias_bc[None], dt_raw, extra_dt,
+        vectors[0:1], vectors[1:2],
+    )
+    decays = jnp.repeat(jnp.exp(logs), width // heads, axis=1)
+    all_logs = lax.all_gather(logs[2], ("ctx", "head")).reshape(n_ctx, n_head, heads)
+
+    steps = heads // STEP_HEADS
+    wide = STEP_HEADS * (width // heads)
+    per_group = group_width // wide
+    tall = pl.BlockSpec((rows, wide), lambda i: (0, i))
+    tall_deep = pl.BlockSpec((deep, wide), lambda i: (0, i))
+    eight = pl.BlockSpec((8, wide), lambda i: (0, i))
+    by_group = pl.BlockSpec((1, state, wide), lambda i: (i // per_group, 0, i % per_group))
+    row_heads = pl.BlockSpec((STEP_HEADS, deep), lambda i: (i, 0))
+
+    def whole(*dims):
+        return pl.BlockSpec(dims, lambda i: (0,) * len(dims))
+
+    grouped = shape((n_head, state, group_width), f32)
+    xc, st_first, summary = pl.pallas_call(
+        states_kernel,
+        grid=(steps,),
+        in_specs=[
+            smem,
+            tall,
+            pl.BlockSpec((RIM, wide), lambda i: (0, i)),
+            pl.BlockSpec((RIM + HALF, wide), lambda i: (0, i)),
+            eight,
+            whole(state, deep),
+            row_heads,
+            eight,
+        ],
+        out_specs=[tall_deep, by_group, by_group],
+        out_shape=[shape((deep, width), bf16), grouped, grouped],
+        compiler_params=params(),
+        cost_estimate=pl.CostEstimate(
+            flops=2 * rows * state * width, bytes_accessed=20 * 2**20, transcendentals=rows * width
+        ),
+        name="states",
+    )(odd, x_in, halo_x, extra_x, par, bt, wt, decays)
+
+    parts = lax.all_to_all(summary, "head", split_axis=0, concat_axis=0, tiled=True)
+
+    g_steps = g.reshape(rows, steps, STEP_HEADS).transpose(1, 0, 2)
+    y_near = pl.pallas_call(
+        diag_kernel,
+        grid=(steps,),
+        in_specs=[
+            smem,
+            tall_deep,
+            whole(5, HALF, HALF),
+            pl.BlockSpec((1, rows, STEP_HEADS), lambda i: (i, 0, 0)),
+            row_heads,
+            row_heads,
+            eight,
+        ],
+        out_specs=tall,
+        out_shape=shape((rows, width), f32),
+        compiler_params=params(),
+        cost_estimate=pl.CostEstimate(
+            flops=10 * 2 * HALF * HALF * width,
+            bytes_accessed=20 * 2**20,
+            transcendentals=5 * HALF * HALF * heads,
+        ),
+        name="diag",
+    )(odd, xc, scores, g_steps, gt, dtt, par)
+
+    own_logs = lax.dynamic_slice_in_dim(all_logs, zed * group_heads, group_heads, 2)
+
+    def lanes_of(log):
+        return jnp.repeat(jnp.exp(log), width // heads)[None, :]
+
+    total = parts[0]
+    for k in range(1, n_head):
+        total = total * lanes_of(own_logs[ctx, k]) + parts[k]
+    seg_logs = own_logs.sum(1)
+    before = jnp.zeros_like(total)
+    span = 1
+    while span < n_ctx:
+        other = lax.ppermute(total, "ctx", [(i, i ^ span) for i in range(n_ctx)])
+        block_logs = seg_logs.reshape(n_ctx // span, span, group_heads).sum(1)
+        block = ctx // span
+        upper = block % 2 == 1
+        own_dec = lanes_of(block_logs[block])
+        other_dec = lanes_of(block_logs[block ^ 1])
+        place = jnp.arange(n_ctx)
+        inside = (place >= block * span) & (place < ctx)
+        lead = lanes_of(jnp.sum(jnp.where(inside[:, None], seg_logs, 0.0), 0))
+        before = jnp.where(upper, other * lead + before, before)
+        total = jnp.where(upper, other * own_dec + total, total * other_dec + other)
+        span *= 2
+    entries = [before]
+    for k in range(n_head - 1):
+        entries.append(entries[-1] * lanes_of(own_logs[ctx, k]) + parts[k])
+    h_in = lax.all_to_all(jnp.stack(entries), "head", split_axis=0, concat_axis=0, tiled=True)
+
+    tile = pl.BlockSpec((HALF, width), lambda i: (i, 0))
+    narrow = pl.BlockSpec((HALF, heads), lambda i: (i, 0))
+    return pl.pallas_call(
+        gate_kernel,
+        grid=(rows // HALF,),
+        in_specs=[
+            smem,
+            tile,
+            pl.BlockSpec((HALF, state), lambda i: (i, 0)),
+            narrow,
+            whole(n_head, state, group_width),
+            whole(n_head, state, group_width),
+            whole(8, width),
+            tile,
+            whole(1, width),
+        ],
+        out_specs=tile,
+        out_shape=shape((rows, width), bf16),
+        scratch_shapes=[pltpu.VMEM((HALF, width), f32)],
+        compiler_params=params(),
+        name="gate",
+    )(odd, y_near, c, ecs, h_in, st_first, decays, z_in, norm_gain[None])
+
+
 def solution(mesh):
     in_specs = (
         P(("ctx", "head"), None),
@@ -129,6 +505,14 @@
         P(),
     )
     out_specs = P(("ctx", "head"), None)
-    return jax.shard_map(
-        per_device, mesh=mesh, in_specs=in_specs, out_specs=out_specs, check_vma=False
-    )
+
+    def run(x_in, *rest):
+        n_ctx, n_head = mesh.shape["ctx"], mesh.shape["head"]
+        rows = x_in.shape[0] // (n_ctx * n_head)
+        fits = 2 * rows == 3 * BLOCK and n_head % 2 == 0 and n_ctx & (n_ctx - 1) == 0
+        body = per_device if fits else per_device_by_heads
+        return jax.shard_map(
+            body, mesh=mesh, in_specs=in_specs, out_specs=out_specs, check_vma=False
+        )(x_in, *rest)
+
+    return run

time: 580 us -> 453 us (0.78)
  local copies, waits for them, and re-layouts: 113 us -> 20.5 us
  Pallas kernels: 0 us -> 68.1 us
  other arithmetic: 72 us -> 14.4 us
  waiting for transfers between devices: 162 us -> 118 us
  blocking collectives: 166 us -> 208 us
  matrix products: 31.2 us -> 0 us
  between operations: 14.5 us -> 0.26 us
    pallas_call x0 -> x4, Pallas kernels: none -> 68.1 us  [the longest x1 25.6 us: per_device(): pl.pallas_call(states_kernel, grid=(steps,), in_specs=[smem, tall, pl.Blo...]
    all_to_all x3 -> x2, waiting for transfers between devices: 130 us -> 68.3 us  [the longest x1 68.3 us: per_device(): lax.all_to_all(jnp.stack(entries), 'head', split_axis=0, concat_axis=0, t...]
    all_gather x1 -> x2, blocking collectives: 151 us -> 208 us  [the longest x1 148 us: per_device(): lax.all_gather(logs[2], ('ctx', 'head')).reshape(n_ctx, n_head, heads)]
    ppermute x1 -> x6, waiting for transfers between devices: 0.01 us -> 49.4 us  [the longest x3 49.4 us: per_device(): other = lax.ppermute(total, 'ctx', [(i, i ^ span) for i in range(n_ctx)])]
    all_gather x1 -> x0, waiting for transfers between devices: 31.5 us -> none  [entering(): everything = jax.tree.map(lambda part: lax.all_gather(part, axis), value)]
    reshape x2, local copies, waits for them, and re-layouts: 33.5 us -> 3.07 us  [the longest x1 2.18 us: per_device(): g_steps = g.reshape(rows, steps, STEP_HEADS).transpose(1, 0, 2)]
    dot_general x3 -> x0, matrix products: 29.4 us -> none  [the longest x1 15.7 us: per_device(): jnp.einsum('chts,cshp->cthp', m_mat, x_blk, preferred_element_type=jnp.fl...]
    all_to_all x3 -> x0, local copies, waits for them, and re-layouts: 26.7 us -> none  [the longest x2 20.1 us: per_device(): lax.all_to_all(y_out.reshape(seg_rows, x_width), 'head', split_axis=0, co...]
  transfers between devices with their start and end apart: 5 -> 8, of which waited for: 2 -> 4; matrix products, arithmetic and copies ran while one was open for 6% -> 4% of each run, Pallas kernels for 0% -> 6%
where the time goes in v1:
time: 453 us; the launch traced here: 452 us
  blocking collectives  208 us (46%)
  waiting for transfers between devices  118 us (26%)
  Pallas kernels  68.1 us (15%)
  starting transfers between devices  22.7 us (5%)
  local copies, waits for them, and re-layouts  20.5 us (5%)
  other arithmetic  14.4 us (3%)
    all_gather x1, blocking collectives, per_device(): lax.all_gather(logs[2], ('ctx', 'head')).reshape(n_ctx, n_head, heads)  148 us
    all_to_all x1, waiting for transfers between devices, per_device(): lax.all_to_all(jnp.stack(entries), 'head', split_axis=0, concat_axis=0, t...  68.3 us
    all_gather x1, blocking collectives, per_device(): table = lax.all_gather(mine, 'head')  60.2 us
    ppermute x3, waiting for transfers between devices, per_device(): other = lax.ppermute(total, 'ctx', [(i, i ^ span) for i in range(n_ctx)])  49.4 us
    pallas_call x1, Pallas kernels, per_device(): pl.pallas_call(states_kernel, grid=(steps,), in_specs=[smem, tall, pl.Blo...  25.6 us
    pallas_call x1, Pallas kernels, per_device(): pl.pallas_call(diag_kernel, grid=(steps,), in_specs=[smem, tall_deep, who...  21.2 us
    pallas_call x1, Pallas kernels, per_device(): pl.pallas_call(gate_kernel, grid=(rows // HALF,), in_specs=[smem, tile, p...  17.6 us
  transfers between devices with their start and end apart: 8, of which 4 were waited for; matrix products, arithmetic and copies ran while one was open for 4% of the time, Pallas kernels for 6%

profile of v1, /device:TPU:0, one launch (start us, length us, event | category | flops | bytes accessed | tf_op | source)
XLA Modules:
  0.0 451.7 jit_solution(11176725114310999100)
XLA Ops:
  0.0 1.0 slice.79
  1.0 0.7 slice.80
  1.8 4.9 %collective-permute-start = (bf16[16,8448]{1,0:T(8,128)(2,1)S(1)}, bf16[16,8448]{1,0:T(8,128)(2,1)S(1)}, u32[]{:S(2)}, u32[]{:S(2)}) collective-permute-start(bf16[16,8448]{1,0:T(8,128)(2,1)S(1)} %pad_maximum_fusion.1), channel_id=1, source_target_pairs={{0,1},{1,2},{2,3},{3,4},{4,5},{5,6},{6,7},{7,8},{8,9},{9,10},{10,1... | collective-permute-start | bytes 811016 | tf_op jit(solution)/shard_map/ppermute | solution.py:342
  6.7 0.9 slice.91
  7.6 0.8 slice.92
  8.4 0.7 pad_maximum_fusion.2
  9.1 4.1 collective-permute-start.2
  13.2 3.3 slice.82
  16.4 1.4 collective-permute-start.1
  18.0 60.2 %all-gather.1 = f32[4,6,2048]{2,1,0:T(8,128)S(1)} all-gather(f32[1,6,2048]{2,1,0:T(8,128)S(1)} %maximum_bitcast_fusion), channel_id=2, replica_groups=mesh['ctx'=8,'head'=4] {'head'}, dimensions={0}, use_global_device_ids=true | all-gather | bytes 245760 | tf_op jit(solution)/shard_map/all_gather | solution.py:334
  78.2 0.1 reshape_squeeze.3
  78.3 0.1 squeeze.44
  78.5 0.1 broadcast_in_dim_reshape.2
  78.7 0.8 fusion.3.par_ref
  79.5 0.6 slice.96.dtb_ref
  80.1 0.7 slice.98.alog_ref
  80.8 1.5 slice.120.ebc_ref
  82.3 1.4 slice.121.edt_ref
  83.7 0.6 slice.119.halo_ref
  84.3 3.6 prep.1
  87.9 0.7 exp.62
  88.6 0.2 broadcast_in_dim.91
  88.8 0.9 reshape.70.dec_ref
  89.7 0.7 slice.112.halo_ref
  90.4 1.4 copy-done
  91.8 25.6 %states.1 = (bf16[512,8192]{1,0:T(8,128)(2,1)}, f32[4,128,2048]{2,1,0:T(8,128)}, f32[4,128,2048]{2,1,0:T(8,128)}) custom-call(s32[1]{0:T(128)} %bitcast.odd_ref, bf16[384,8192]{1,0:T(8,128)(2,1)} %x_ref.1, bf16[16,8192]{1,0:T(8,128)(2,1)} %slice.112.halo_ref, bf16[144,8192]{1,0:T(8,128)(2,1)} %copy-done, f32[8,8192]{1,0:T(8,128)} %fusion.3.par_ref, ...), custom_call_target="tpu_custom_call" | custom-call | flops 805306368 | bytes 20971520 | tf_op jit(solution)/shard_map/states/pallas_call | solution.py:391
  117.4 5.4 %all-to-all-start = ((f32[4,128,2048]{2,1,0:T(8,128)}), f32[4,128,2048]{2,1,0:T(8,128)}, u32[]{:S(2)}, u32[]{:S(2)}) async-start(f32[4,128,2048]{2,1,0:T(8,128)} %get-tuple-element.27), calls=%async_computation | async-start | bytes 8388608 | tf_op jit(solution)/shard_map/all_to_all | solution.py:413
  122.8 0.7 slice_bitcast_fusion.8
  123.5 147.8 %all-gather.2 = f32[32,1,128]{2,1,0:T(1,128)S(1)} all-gather(f32[1,1,128]{2,1,0:T(1,128)S(1)} %slice_bitcast_fusion.8), channel_id=1, replica_groups=mesh['ctx'=8,'head'=4] {'ctx','head'}, dimensions={0}, use_global_device_ids=true | all-gather | bytes 16896 | tf_op jit(solution)/shard_map/all_gather | solution.py:376
  271.3 0.1 exponential_bitcast_fusion
  271.8 2.5 fusion
  274.4 0.1 dynamic-slice_reduce_fusion
  274.8 2.2 collective-permute-done.3
  277.0 2.7 add_select_fusion.3
  280.2 24.8 %collective-permute-done.4 = f32[128,2048]{1,0:T(8,128)S(1)} collective-permute-done((f32[128,2048]{1,0:T(8,128)S(1)}, f32[128,2048]{1,0:T(8,128)S(1)}, u32[]{:S(2)}, u32[]{:S(2)}) %collective-permute-start.4) | collective-permute-done | bytes 1048608 | tf_op jit(solution)/shard_map/ppermute | solution.py:451
  305.0 1.2 add_select_fusion.2
  306.2 1.5 collective-permute-start.5
  307.7 0.1 select_reduce_fusion.2
  308.4 22.4 %collective-permute-done.5 = f32[128,2048]{1,0:T(8,128)S(1)} collective-permute-done((f32[128,2048]{1,0:T(8,128)}, f32[128,2048]{1,0:T(8,128)S(1)}, u32[]{:S(2)}, u32[]{:S(2)}) %collective-permute-start.5) | collective-permute-done | bytes 1048608 | tf_op jit(solution)/shard_map/ppermute | solution.py:451
  330.8 1.7 fusion.1
  332.5 2.2 add_bitcast_fusion
  334.7 2.3 pad_maximum_fusion
  337.0 5.2 %all-to-all-start.1 = ((f32[4,128,2048]{2,1,0:T(8,128)}), f32[4,128,2048]{2,1,0:T(8,128)}, u32[]{:S(2)}, u32[]{:S(2)}) async-start(f32[4,128,2048]{2,1,0:T(8,128)} %pad_maximum_fusion), calls=%async_computation.1 | async-start | bytes 8388608 | tf_op jit(solution)/shard_map/all_to_all | solution.py:466
  342.2 0.1 copy.16
  342.3 2.2 copy.17
  344.5 21.2 %diag.1.y_ref = f32[384,8192]{1,0:T(8,128)} custom-call(s32[1]{0:T(128)} %bitcast.odd_ref, bf16[512,8192]{1,0:T(8,128)(2,1)} %get-tuple-element.20.xc_ref, f32[5,128,128]{2,1,0:T(8,128)} %get-tuple-element.21.s_ref, f32[16,384,8]{2,1,0:T(8,128)} %bitcast.80, f32[128,512]{1,0:T(8,128)} %get-tuple-element.23.gt_ref, f32[128,512]{1,0:T(8,128)} %get-tuple-element.24.dtt_ref, ...), custom_call_target="tpu_custom_call" | custom-call | flops 2684354560 | bytes 20971520 | tf_op jit(solution)/shard_map/diag/pallas_call | solution.py:416
  365.7 68.3 %all-to-all-done.1.h_ref = f32[4,128,2048]{2,1,0:T(8,128)} async-done(((f32[4,128,2048]{2,1,0:T(8,128)}), f32[4,128,2048]{2,1,0:T(8,128)}, u32[]{:S(2)}, u32[]{:S(2)}) %all-to-all-start.1) | async-done | bytes 4194336 | tf_op jit(solution)/shard_map/all_to_all | solution.py:466
  434.1 17.6 %gate.1 = bf16[384,8192]{1,0:T(8,128)(2,1)} custom-call(s32[1]{0:T(128)} %bitcast.odd_ref, f32[384,8192]{1,0:T(8,128)} %diag.1.y_ref, bf16[384,128]{1,0:T(8,128)(2,1)} %get-tuple-element.25.c_ref, f32[384,128]{1,0:T(8,128)} %get-tuple-element.26.ecs_ref, f32[4,128,2048]{2,1,0:T(8,128)} %all-to-all-done.1.h_ref, f32[4,128,2048]{2,1,0:T(8,128)} %get-tuple-element.28.st_ref, ...), custom_call_target="tpu_custom_call" | custom-call | tf_op jit(solution)/shard_map/gate/pallas_call | solution.py:470
  (58 shorter events, 2.2 us)
Async XLA Ops:
  0.0 17.9 %copy-start.6 = (f32[32]{0:T(128)S(1)}, f32[32]{0:T(128)}, u32[]{:S(2)}) copy-start(f32[32]{0:T(128)} %param.20) | copy-start | bytes 388
  0.0 17.9 %copy-start.5 = (f32[32]{0:T(128)S(1)}, f32[32]{0:T(128)}, u32[]{:S(2)}) copy-start(f32[32]{0:T(128)} %param.21) | copy-start | bytes 388
  0.0 17.9 %copy-start.4 = (f32[32]{0:T(128)S(1)}, f32[32]{0:T(128)}, u32[]{:S(2)}) copy-start(f32[32]{0:T(128)} %param.22) | copy-start | bytes 388
  0.0 18.0 %copy-start.3 = (f32[2048]{0:T(1024)S(1)}, f32[2048]{0:T(1024)}, u32[]{:S(2)}) copy-start(f32[2048]{0:T(1024)} %param.17) | copy-start | bytes 24580
  0.0 18.0 %copy-start.2 = (f32[4,2048]{1,0:T(4,128)S(1)}, f32[4,2048]{1,0:T(4,128)}, u32[]{:S(2)}) copy-start(f32[4,2048]{1,0:T(4,128)} %param.16) | copy-start | bytes 98308
  1.8 81.9 %collective-permute-start = (bf16[16,8448]{1,0:T(8,128)(2,1)S(1)}, bf16[16,8448]{1,0:T(8,128)(2,1)S(1)}, u32[]{:S(2)}, u32[]{:S(2)}) collective-permute-start(bf16[16,8448]{1,0:T(8,128)(2,1)S(1)} %pad_maximum_fusion.1), channel_id=1, source_target_pairs={{0,1},{1,2},{2,3},{3,4},{4,5},{5,6},{6,7},{7,8},{8,9},{9,10},{10,1... | collective-permute-start | bytes 811016 | tf_op jit(solution)/shard_map/ppermute | solution.py:342
  9.1 71.7 %collective-permute-start.2 = (bf16[144,384]{1,0:T(8,128)(2,1)}, bf16[144,384]{1,0:T(8,128)(2,1)}, u32[]{:S(2)}, u32[]{:S(2)}) collective-permute-start(bf16[144,384]{1,0:T(8,128)(2,1)} %pad_maximum_fusion.2), channel_id=1, source_target_pairs={{0,1},{2,3},{4,5},{6,7},{8,9},{10,11},{12,13},{14,15},{16,17},{18,... | collective-permute-start | bytes 331784 | tf_op jit(solution)/shard_map/ppermute | solution.py:347
  16.4 74.0 %collective-permute-start.1 = (bf16[144,8192]{1,0:T(8,128)(2,1)}, bf16[144,8192]{1,0:T(8,128)(2,1)S(1)}, u32[]{:S(2)}, u32[]{:S(2)}) collective-permute-start(bf16[144,8192]{1,0:T(8,128)(2,1)} %slice.82), channel_id=1, source_target_pairs={{0,1},{2,3},{4,5},{6,7},{8,9},{10,11},{12,13},{14,15},{16,17},{18,... | collective-permute-start | bytes 7077896 | tf_op jit(solution)/shard_map/ppermute | solution.py:346
  90.4 1.4 copy-start
  117.4 154.4 %all-to-all-start = ((f32[4,128,2048]{2,1,0:T(8,128)}), f32[4,128,2048]{2,1,0:T(8,128)}, u32[]{:S(2)}, u32[]{:S(2)}) async-start(f32[4,128,2048]{2,1,0:T(8,128)} %get-tuple-element.27), calls=%async_computation | async-start | bytes 8388608 | tf_op jit(solution)/shard_map/all_to_all | solution.py:413
  274.3 2.7 collective-permute-start.3
  279.8 25.3 %collective-permute-start.4 = (f32[128,2048]{1,0:T(8,128)S(1)}, f32[128,2048]{1,0:T(8,128)S(1)}, u32[]{:S(2)}, u32[]{:S(2)}) collective-permute-start(f32[128,2048]{1,0:T(8,128)S(1)} %add_select_fusion.3), channel_id=1, source_target_pairs={{0,8},{4,12},{8,0},{12,4},{16,24},{20,28},{24,16},{28,20},{1,9},{5... | collective-permute-start | bytes 3145736 | tf_op jit(solution)/shard_map/ppermute | solution.py:451
  306.2 24.6 %collective-permute-start.5 = (f32[128,2048]{1,0:T(8,128)}, f32[128,2048]{1,0:T(8,128)S(1)}, u32[]{:S(2)}, u32[]{:S(2)}) collective-permute-start(f32[128,2048]{1,0:T(8,128)} %add_select_fusion.2), channel_id=1, source_target_pairs={{0,16},{4,20},{8,24},{12,28},{16,0},{20,4},{24,8},{28,12},{1,17},{... | collective-permute-start | bytes 3145736 | tf_op jit(solution)/shard_map/ppermute | solution.py:451
  337.0 5.2 %copy-start.1 = (f32[384,128]{1,0:T(8,128)S(1)}, f32[384,128]{1,0:T(8,128)}, u32[]{:S(2)}) copy-start(f32[384,128]{1,0:T(8,128)} %get-tuple-element.22) | copy-start | bytes 589828
  337.0 97.1 %all-to-all-start.1 = ((f32[4,128,2048]{2,1,0:T(8,128)}), f32[4,128,2048]{2,1,0:T(8,128)}, u32[]{:S(2)}, u32[]{:S(2)}) async-start(f32[4,128,2048]{2,1,0:T(8,128)} %pad_maximum_fusion), calls=%async_computation.1 | async-start | bytes 8388608 | tf_op jit(solution)/shard_map/all_to_all | solution.py:466

commit v2 on v1

--- a/solution.py
+++ b/solution.py
@@ -196,43 +196,63 @@
     dtt_ref[...] = dt.T
     wt_ref[...] = weight.T
     log_ref[...] = jnp.concatenate(
-        [g_cut, g_end - g_cut, jnp.where(odd, g_end, g_cut), jnp.zeros((5, g.shape[1]))], 0
-    )
-
-
-def states_kernel(
-    odd_ref, x_ref, halo_ref, ex_ref, par_ref, bt_ref, wt_ref, dec_ref, xc_ref, st_ref, sum_ref
+        [
+            jnp.exp(g_cut),
+            jnp.exp(g_end - g_cut),
+            jnp.where(odd, g_end, g_cut),
+            jnp.zeros((5, g.shape[1])),
+        ],
+        0,
+    )
+
+
+def weighted(bt, wt, xc, pair, left):
+    n = bt.shape[0]
+    both = [(bt * wt[2 * pair + k : 2 * pair + k + 1]).astype(jnp.bfloat16) for k in range(2)]
+    full = jnp.dot(jnp.concatenate(both, 0), xc, preferred_element_type=jnp.float32)
+    return jnp.where(left, full[:n], full[n:])
+
+
+def own_kernel(odd_ref, x_ref, halo_ref, par_ref, bt_ref, wt_ref, xc_ref, qa_ref, qb_ref):
+    odd = odd_ref[0] == 1
+    par = par_ref[...]
+    xc = rows_conv(halo_ref[...], x_ref[...], par[0:4], par[4:5])
+    xc_ref[...] = xc
+    bt = bt_ref[...].astype(jnp.float32)
+    wt = wt_ref[...]
+    left = lax.broadcasted_iota(jnp.int32, (bt.shape[0], 128), 1) < 64
+    for pair in range(STEP_HEADS // 2):
+        lanes = slice(pair * 128, pair * 128 + 128)
+        parts = []
+        for i in range(3):
+            at, cols = slice(i * HALF, (i + 1) * HALF), slice((i + 1) * HALF, (i + 2) * HALF)
+            parts.append(weighted(bt[:, cols], wt[:, cols], xc[at, lanes], pair, left))
+        qa_ref[0, 0, :, lanes] = parts[0] + jnp.where(odd, 0.0, parts[1])
+        qb_ref[0, 0, :, lanes] = jnp.where(odd, parts[1] + parts[2], 0.0)
+
+
+def extra_kernel(
+    odd_ref, ex_ref, par_ref, bt_ref, wt_ref, dec_ref, qa_ref, qb_ref, xc_ref, st_ref, sum_ref
 ):
     odd = odd_ref[0] == 1
     par = par_ref[...]
     ex = ex_ref[...].astype(jnp.float32)
-    xc_ref[:HALF] = rows_conv(ex[:RIM], ex[RIM:], par[0:4], par[4:5])
-    xc_ref[HALF:] = rows_conv(halo_ref[...], x_ref[...], par[0:4], par[4:5])
-    bt = bt_ref[...].astype(jnp.float32)
-    wt = wt_ref[...]
+    xc = rows_conv(ex[:RIM], ex[RIM:], par[0:4], par[4:5])
+    xc_ref[...] = xc
+    bt = bt_ref[...].astype(jnp.float32)[:, :HALF]
+    wt = wt_ref[...][:, :HALF]
     n = bt.shape[0]
     left = lax.broadcasted_iota(jnp.int32, (n, 128), 1) < 64
     for pair in range(STEP_HEADS // 2):
         lanes = slice(pair * 128, pair * 128 + 128)
-        parts = []
-        for i in range(4):
-            cols = slice(i * HALF, (i + 1) * HALF)
-            both = jnp.concatenate(
-                [
-                    (bt[:, cols] * wt[2 * pair + k : 2 * pair + k + 1, cols]).astype(jnp.bfloat16)
-                    for k in range(2)
-                ],
-                0,
-            )
-            full = jnp.dot(both, xc_ref[cols, lanes], preferred_element_type=jnp.float32)
-            parts.append(jnp.where(left, full[:n], full[n:]))
-        st_first = parts[1] + jnp.where(odd, parts[0], parts[2])
-        both_blocks = st_first * dec_ref[1:2, lanes] + (parts[2] + parts[3])
-        st_ref[0, :, lanes] = st_first
-        sum_ref[0, :, lanes] = jnp.where(odd, both_blocks, st_first)
-
-
-def diag_kernel(odd_ref, xc_ref, s_ref, g_ref, gt_ref, dtt_ref, par_ref, y_ref):
+        st_first = qa_ref[0, 0, :, lanes] + weighted(bt, wt, xc[:, lanes], pair, left)
+        both_blocks = st_first * dec_ref[1:2, lanes] + qb_ref[0, 0, :, lanes]
+        st_ref[0, 0, :, lanes] = st_first
+        sum_ref[0, 0, :n, lanes] = jnp.where(odd, both_blocks, st_first)
+    sum_ref[0, 0, n:, :] = jnp.broadcast_to(dec_ref[2:3, :], (8, dec_ref.shape[1]))
+
+
+def diag_kernel(odd_ref, xc_ref, xe_ref, s_ref, g_ref, gt_ref, dtt_ref, par_ref, y_ref):
     shift = odd_ref[0]
     odd = shift == 1
     g, gt, dtt = g_ref[0], gt_ref[...], dtt_ref[...]
@@ -245,10 +265,12 @@
     behind = [slice(i * HALF, (i + 1) * HALF) for i in range(4)]
     gt_off = jnp.where(odd, gt[:, behind[2]], gt[:, behind[1]])
     dtt_off = jnp.where(odd, dtt[:, behind[2]], dtt[:, behind[1]])
-    x_off = xc_ref[pl.ds(pl.multiple_of(HALF + shift * HALF, HALF), HALF), :]
-    tiles = [(g[subs[i]], gt[:, at], dtt[:, at], xc_ref[at, :]) for i, at in enumerate(behind[1:])]
+    x_off = xc_ref[pl.ds(pl.multiple_of(shift * HALF, HALF), HALF), :]
+    tiles = [
+        (g[sub], gt[:, at], dtt[:, at], xc_ref[sub, :]) for sub, at in zip(subs, behind[1:])
+    ]
     tiles.append((g_off, gt_off, dtt_off, x_off))
-    tiles.append((g[subs[0]], gt[:, behind[0]], dtt[:, behind[0]], xc_ref[behind[0], :]))
+    tiles.append((g[subs[0]], gt[:, behind[0]], dtt[:, behind[0]], xe_ref[...]))
     for pair in range(STEP_HEADS // 2):
         lanes = slice(pair * 128, pair * 128 + 128)
         results = []
@@ -279,20 +301,22 @@
 
 
 def gate_kernel(
-    odd_ref, y_ref, c_ref, ecs_ref, h_ref, st_ref, dec_ref, z_ref, gain_ref, out_ref, held
+    odd_ref, y_ref, c_ref, ecs_ref, ha_ref, hb_ref, st_ref, dec_ref, z_ref, gain_ref, out_ref, held
 ):
     early = pl.program_id(0) < 2 - odd_ref[0]
     c = c_ref[...]
     ecs = ecs_ref[...]
     left = lax.broadcasted_iota(jnp.int32, (HALF, 128), 1) < 64
-    groups, _, width = h_ref.shape
+    groups, _, part = ha_ref.shape
+    width = 2 * part
     wide = STEP_HEADS * 64
     square = jnp.zeros((HALF, 128), jnp.float32)
     for start in range(0, groups * width, wide):
         group, off = divmod(start, width)
+        side, off = divmod(off, part)
         cols = slice(off, off + wide)
-        h = h_ref[group, :, cols]
-        later = h * dec_ref[0:1, start : start + wide] + st_ref[group, :, cols]
+        h = (ha_ref, hb_ref)[side][group, :, cols]
+        later = h * dec_ref[0:1, start : start + wide] + st_ref[side, group, :, cols]
         hb = jnp.where(early, h, later).astype(jnp.bfloat16)
         far = jnp.dot(c, hb, preferred_element_type=jnp.float32)
         for pair in range(STEP_HEADS // 2):
@@ -332,21 +356,22 @@
     small = jnp.pad(small, (0, group_width - small.shape[0]))
     mine = jnp.concatenate([conv_x, bias_x[None], small[None]], 0)
     table = lax.all_gather(mine, "head")
+    count = n_ctx * n_head
+    rim = jnp.concatenate([x_in[-RIM:], bc_in[-RIM:]], 1)
+    rim = lax.ppermute(rim, ("ctx", "head"), [(i, i + 1) for i in range(count - 1)])
+    last = rows - HALF - RIM
+    to_odd = [(i, i + 1) for i in range(0, n_head, 2)]
+    extra_small = lax.ppermute(jnp.concatenate([bc_in[last:], dt_raw[last:]], 1), "head", to_odd)
+    deep = rows + HALF
+    tail, rim, table, extra_small = lax.optimization_barrier((x_in[last:], rim, table, extra_small))
+    extra_x = lax.ppermute(tail, "head", to_odd)
+    halo_x, halo_bc = rim[:, :width], rim[:, width:]
+    extra_bc, extra_dt = extra_small[:, : 2 * state], extra_small[:, 2 * state :]
     par = jnp.concatenate([table[g] for g in range(n_head)], 1)
     vectors = table[:, 5, : 3 * group_heads].reshape(n_head, 3, group_heads)
     vectors = vectors.transpose(1, 0, 2).reshape(3, heads)
     skip = jnp.repeat(vectors[2], width // heads)
     par = jnp.concatenate([par[:5], skip[None], jnp.zeros((2, width), f32)], 0)
-    count = n_ctx * n_head
-    rim = jnp.concatenate([x_in[-RIM:], bc_in[-RIM:]], 1)
-    rim = lax.ppermute(rim, ("ctx", "head"), [(i, i + 1) for i in range(count - 1)])
-    halo_x, halo_bc = rim[:, :width], rim[:, width:]
-    last = rows - HALF - RIM
-    to_odd = [(i, i + 1) for i in range(0, n_head, 2)]
-    extra_x = lax.ppermute(x_in[last:], "head", to_odd)
-    extra_small = lax.ppermute(jnp.concatenate([bc_in[last:], dt_raw[last:]], 1), "head", to_odd)
-    extra_bc, extra_dt = extra_small[:, : 2 * state], extra_small[:, 2 * state :]
-    deep = rows + HALF
 
     smem = pl.BlockSpec(memory_space=pltpu.SMEM)
     vmem = pl.BlockSpec(memory_space=pltpu.VMEM)
@@ -372,45 +397,111 @@
         odd, bc_in, halo_bc, extra_bc, conv_bc, bias_bc[None], dt_raw, extra_dt,
         vectors[0:1], vectors[1:2],
     )
-    decays = jnp.repeat(jnp.exp(logs), width // heads, axis=1)
-    all_logs = lax.all_gather(logs[2], ("ctx", "head")).reshape(n_ctx, n_head, heads)
+    decays = jnp.repeat(logs, width // heads, axis=1)
 
     steps = heads // STEP_HEADS
     wide = STEP_HEADS * (width // heads)
     per_group = group_width // wide
     tall = pl.BlockSpec((rows, wide), lambda i: (0, i))
-    tall_deep = pl.BlockSpec((deep, wide), lambda i: (0, i))
     eight = pl.BlockSpec((8, wide), lambda i: (0, i))
-    by_group = pl.BlockSpec((1, state, wide), lambda i: (i // per_group, 0, i % per_group))
+    part = group_width // 2
+    per_part = part // wide
+
+    def by_group(depth):
+        return pl.BlockSpec(
+            (1, 1, depth, wide),
+            lambda i: (i // per_part % 2, i // per_group, 0, i % per_part),
+        )
+
     row_heads = pl.BlockSpec((STEP_HEADS, deep), lambda i: (i, 0))
 
     def whole(*dims):
         return pl.BlockSpec(dims, lambda i: (0,) * len(dims))
 
-    grouped = shape((n_head, state, group_width), f32)
-    xc, st_first, summary = pl.pallas_call(
-        states_kernel,
+    def grouped(depth):
+        return shape((2, n_head, depth, part), f32)
+
+    xc, q_first, q_second = pl.pallas_call(
+        own_kernel,
         grid=(steps,),
         in_specs=[
             smem,
             tall,
             pl.BlockSpec((RIM, wide), lambda i: (0, i)),
+            eight,
+            whole(state, deep),
+            row_heads,
+        ],
+        out_specs=[tall, by_group(state), by_group(state)],
+        out_shape=[shape((rows, width), bf16), grouped(state), grouped(state)],
+        compiler_params=params(),
+        cost_estimate=pl.CostEstimate(
+            flops=2 * rows * state * width, bytes_accessed=20 * 2**20, transcendentals=rows * width
+        ),
+        name="own",
+    )(odd, x_in, halo_x, par, bt, wt)
+    half_tall = pl.BlockSpec((HALF, wide), lambda i: (0, i))
+    xe, st_first, summary = pl.pallas_call(
+        extra_kernel,
+        grid=(steps,),
+        in_specs=[
+            smem,
             pl.BlockSpec((RIM + HALF, wide), lambda i: (0, i)),
             eight,
             whole(state, deep),
             row_heads,
             eight,
-        ],
-        out_specs=[tall_deep, by_group, by_group],
-        out_shape=[shape((deep, width), bf16), grouped, grouped],
+            by_group(state),
+            by_group(state),
+        ],
+        out_specs=[half_tall, by_group(state), by_group(state + 8)],
+        out_shape=[shape((HALF, width), bf16), grouped(state), grouped(state + 8)],
         compiler_params=params(),
         cost_estimate=pl.CostEstimate(
-            flops=2 * rows * state * width, bytes_accessed=20 * 2**20, transcendentals=rows * width
+            flops=2 * HALF * state * width, bytes_accessed=20 * 2**20, transcendentals=HALF * width
         ),
-        name="states",
-    )(odd, x_in, halo_x, extra_x, par, bt, wt, decays)
-
-    parts = lax.all_to_all(summary, "head", split_axis=0, concat_axis=0, tiled=True)
+        name="extra",
+    )(odd, extra_x, par, bt, wt, decays, q_first, q_second)
+
+    def exchange(value):
+        return lax.all_to_all(value, "head", split_axis=0, concat_axis=0, tiled=True)
+
+    def scan(parts):
+        logs = [parts[k, state] for k in range(n_head)]
+        total, total_log = parts[0, :state], logs[0]
+        for k in range(1, n_head):
+            total = total * jnp.exp(logs[k])[None] + parts[k, :state]
+            total_log = total_log + logs[k]
+        before, before_log = jnp.zeros_like(total), jnp.zeros_like(total_log)
+        span = 1
+        while span < n_ctx:
+            sent = jnp.concatenate([total, jnp.broadcast_to(total_log[None], (8, part))], 0)
+            got = lax.ppermute(sent, "ctx", [(i, i ^ span) for i in range(n_ctx)])
+            other, other_log = got[:state], got[state]
+            upper = ctx // span % 2 == 1
+            before = jnp.where(upper, other * jnp.exp(before_log)[None] + before, before)
+            before_log = jnp.where(upper, other_log + before_log, before_log)
+            total = jnp.where(
+                upper,
+                other * jnp.exp(total_log)[None] + total,
+                total * jnp.exp(other_log)[None] + other,
+            )
+            total_log = total_log + other_log
+            span *= 2
+        entries = [before]
+        for k in range(n_head - 1):
+            entries.append(entries[-1] * jnp.exp(logs[k])[None] + parts[k, :state])
+        return jnp.stack(entries)
+
+    parts_a = exchange(summary[0])
+    parts_a, later = lax.optimization_barrier((parts_a, summary[1]))
+    parts_b = exchange(later)
+    entries_a = scan(parts_a)
+    entries_a, parts_b = lax.optimization_barrier((entries_a, parts_b))
+    h_a = exchange(entries_a)
+    entries_b = scan(parts_b)
+    entries_b, h_a = lax.optimization_barrier((entries_b, h_a))
+    h_b = exchange(entries_b)
 
     g_steps = g.reshape(rows, steps, STEP_HEADS).transpose(1, 0, 2)
     y_near = pl.pallas_call(
@@ -418,7 +509,8 @@
         grid=(steps,),
         in_specs=[
             smem,
-            tall_deep,
+            tall,
+            half_tall,
             whole(5, HALF, HALF),
             pl.BlockSpec((1, rows, STEP_HEADS), lambda i: (i, 0, 0)),
             row_heads,
@@ -434,36 +526,7 @@
             transcendentals=5 * HALF * HALF * heads,
         ),
         name="diag",
-    )(odd, xc, scores, g_steps, gt, dtt, par)
-
-    own_logs = lax.dynamic_slice_in_dim(all_logs, zed * group_heads, group_heads, 2)
-
-    def lanes_of(log):
-        return jnp.repeat(jnp.exp(log), width // heads)[None, :]
-
-    total = parts[0]
-    for k in range(1, n_head):
-        total = total * lanes_of(own_logs[ctx, k]) + parts[k]
-    seg_logs = own_logs.sum(1)
-    before = jnp.zeros_like(total)
-    span = 1
-    while span < n_ctx:
-        other = lax.ppermute(total, "ctx", [(i, i ^ span) for i in range(n_ctx)])
-        block_logs = seg_logs.reshape(n_ctx // span, span, group_heads).sum(1)
-        block = ctx // span
-        upper = block % 2 == 1
-        own_dec = lanes_of(block_logs[block])
-        other_dec = lanes_of(block_logs[block ^ 1])
-        place = jnp.arange(n_ctx)
-        inside = (place >= block * span) & (place < ctx)
-        lead = lanes_of(jnp.sum(jnp.where(inside[:, None], seg_logs, 0.0), 0))
-        before = jnp.where(upper, other * lead + before, before)
-        total = jnp.where(upper, other * own_dec + total, total * other_dec + other)
-        span *= 2
-    entries = [before]
-    for k in range(n_head - 1):
-        entries.append(entries[-1] * lanes_of(own_logs[ctx, k]) + parts[k])
-    h_in = lax.all_to_all(jnp.stack(entries), "head", split_axis=0, concat_axis=0, tiled=True)
+    )(odd, xc, xe, scores, g_steps, gt, dtt, par)
 
     tile = pl.BlockSpec((HALF, width), lambda i: (i, 0))
     narrow = pl.BlockSpec((HALF, heads), lambda i: (i, 0))
@@ -475,8 +538,9 @@
             tile,
             pl.BlockSpec((HALF, state), lambda i: (i, 0)),
             narrow,
-            whole(n_head, state, group_width),
-            whole(n_head, state, group_width),
+            whole(n_head, state, part),
+            whole(n_head, state, part),
+            whole(2, n_head, state, part),
             whole(8, width),
             tile,
             whole(1, width),
@@ -486,7 +550,7 @@
         scratch_shapes=[pltpu.VMEM((HALF, width), f32)],
         compiler_params=params(),
         name="gate",
-    )(odd, y_near, c, ecs, h_in, st_first, decays, z_in, norm_gain[None])
+    )(odd, y_near, c, ecs, h_a, h_b, st_first, decays, z_in, norm_gain[None])
 
 
 def solution(mesh):

time: 453 us -> 341 us (0.75)
  blocking collectives: 208 us -> 68.9 us
  Pallas kernels: 68.1 us -> 78.6 us
  waiting for transfers between devices: 118 us -> 125 us
  starting transfers between devices: 22.7 us -> 29.3 us
    all_gather x1 -> x0, blocking collectives: 148 us -> none  [per_device(): lax.all_gather(logs[2], ('ctx', 'head')).reshape(n_ctx, n_head, heads)]
    all_to_all x0 -> x1, blocking collectives: none -> 54.8 us  [exchange(): lax.all_to_all(value, 'head', split_axis=0, concat_axis=0, tiled=True)]
    all_gather x1, blocking collectives: 60.2 us -> 14.1 us  [per_device(): table = lax.all_gather(mine, 'head')]
    ppermute x4 -> x7, waiting for transfers between devices: 49.4 us -> 70.3 us  [the longest x6 52.7 us: scan(): got = lax.ppermute(sent, 'ctx', [(i, i ^ span) for i in range(n_ctx)])]
    all_to_all x2 -> x3, waiting for transfers between devices: 68.3 us -> 55.1 us  [exchange(): lax.all_to_all(value, 'head', split_axis=0, concat_axis=0, tiled=True)]
    pallas_call x2 -> x3, Pallas kernels: 46.8 us -> 57.3 us  [the longest x1 21.2 us: per_device(): pl.pallas_call(diag_kernel, grid=(steps,), in_specs=[smem, tall, half_tal...]
    ppermute x4 -> x7, starting transfers between devices: 3.09 us -> 8.99 us  [the longest x6 6.21 us: scan(): got = lax.ppermute(sent, 'ctx', [(i, i ^ span) for i in range(n_ctx)])]
    all_to_all x2 -> x3, starting transfers between devices: 10.6 us -> 11.9 us  [exchange(): lax.all_to_all(value, 'head', split_axis=0, concat_axis=0, tiled=True)]
  transfers between devices with their start and end apart: 8 -> 12, of which waited for: 4 -> 8; matrix products, arithmetic and copies ran while one was open for 4% -> 8% of each run, Pallas kernels for 6% -> 13%
where the time goes in v2:
time: 341 us; the launch traced here: 339 us
  waiting for transfers between devices  125 us (37%)
  Pallas kernels  78.6 us (23%)
  blocking collectives  68.9 us (20%)
  starting transfers between devices  29.3 us (9%)
  local copies, waits for them, and re-layouts  21 us (6%)
  other arithmetic  15.2 us (4%)
    all_to_all x3, waiting for transfers between devices, exchange(): lax.all_to_all(value, 'head', split_axis=0, concat_axis=0, tiled=True)  55.1 us
    all_to_all x1, blocking collectives, exchange(): lax.all_to_all(value, 'head', split_axis=0, concat_axis=0, tiled=True)  54.8 us
    ppermute x6, waiting for transfers between devices, scan(): got = lax.ppermute(sent, 'ctx', [(i, i ^ span) for i in range(n_ctx)])  52.7 us
    pallas_call x1, Pallas kernels, per_device(): pl.pallas_call(diag_kernel, grid=(steps,), in_specs=[smem, tall, half_tal...  21.2 us
    pallas_call x1, Pallas kernels, per_device(): pl.pallas_call(own_kernel, grid=(steps,), in_specs=[smem, tall, pl.BlockS...  20 us
    pallas_call x1, Pallas kernels, per_device(): pl.pallas_call(gate_kernel, grid=(rows // HALF,), in_specs=[smem, tile, p...  17.6 us
    ppermute x1, waiting for transfers between devices, per_device(): extra_x = lax.ppermute(tail, 'head', to_odd)  17.6 us
    pallas_call x1, Pallas kernels, per_device(): pl.pallas_call(extra_kernel, grid=(steps,), in_specs=[smem, pl.BlockSpec(...  16.1 us
  transfers between devices with their start and end apart: 12, of which 8 were waited for; matrix products, arithmetic and copies ran while one was open for 8% of the time, Pallas kernels for 13%

profile of v2, /device:TPU:0, one launch (start us, length us, event | category | flops | bytes accessed | tf_op | source)
XLA Modules:
  0.0 338.8 jit_solution(17728855496222786500)
XLA Ops:
  0.0 1.0 slice.152
  1.0 0.7 slice.153
  1.7 4.9 %collective-permute-start = (bf16[16,8448]{1,0:T(8,128)(2,1)S(1)}, bf16[16,8448]{1,0:T(8,128)(2,1)S(1)}, u32[]{:S(2)}, u32[]{:S(2)}) collective-permute-start(bf16[16,8448]{1,0:T(8,128)(2,1)S(1)} %pad_maximum_fusion.8), channel_id=1, source_target_pairs={{0,1},{1,2},{2,3},{3,4},{4,5},{5,6},{6,7},{7,8},{8,9},{9,10},{10,1... | collective-permute-start | bytes 811016 | tf_op jit(solution)/shard_map/ppermute | solution.py:361
  6.6 0.9 slice.154
  7.5 0.8 slice.155
  8.3 3.5 %collective-permute-start.1 = (bf16[144,384]{1,0:T(8,128)(2,1)S(1)}, bf16[144,384]{1,0:T(8,128)(2,1)S(1)}, u32[]{:S(2)}, u32[]{:S(2)}) collective-permute-start(bf16[144,384]{1,0:T(8,128)(2,1)S(1)} %pad_maximum_fusion.9), channel_id=1, source_target_pairs={{0,1},{2,3},{4,5},{6,7},{8,9},{10,11},{12,13},{14,15},{16,17},{18,... | collective-permute-start | bytes 331784 | tf_op jit(solution)/shard_map/ppermute | solution.py:364
  11.8 0.8 select_maximum_fusion.3
  12.6 0.8 maximum_bitcast_fusion
  13.4 3.3 slice.151
  16.7 14.1 %all-gather.1 = f32[4,6,2048]{2,1,0:T(8,128)S(1)} all-gather(f32[1,6,2048]{2,1,0:T(8,128)S(1)} %maximum_bitcast_fusion), channel_id=2, replica_groups=mesh['ctx'=8,'head'=4] {'head'}, dimensions={0}, use_global_device_ids=true | all-gather | bytes 245760 | tf_op jit(solution)/shard_map/all_gather | solution.py:358
  30.9 2.8 collective-permute-start.2
  35.6 0.7 slice.156.halo_ref
  37.8 3.7 %prep.1 = (bf16[384,128]{1,0:T(8,128)(2,1)}, bf16[128,512]{1,0:T(8,128)(2,1)}, f32[5,128,128]{2,1,0:T(8,128)}, f32[384,128]{1,0:T(8,128)}, f32[128,512]{1,0:T(8,...) custom-call(s32[1]{0:T(128)} %bitcast.odd_ref, ...), custom_call_target="tpu_custom_call" | custom-call | tf_op jit(solution)/shard_map/prep/pallas_call | solution.py:379
  41.5 0.9 broadcast_in_dim.39
  42.3 0.9 reshape.207.dec_ref
  43.2 0.8 fusion.7.par_ref
  44.0 20.0 %own.1 = (bf16[384,8192]{1,0:T(8,128)(2,1)}, f32[2,4,128,1024]{3,2,1,0:T(8,128)}, f32[2,4,128,1024]{3,2,1,0:T(8,128)}) custom-call(s32[1]{0:T(128)} %bitcast.odd_ref, bf16[384,8192]{1,0:T(8,128)(2,1)} %x_ref.1, bf16[16,8192]{1,0:T(8,128)(2,1)} %slice.156.halo_ref, f32[8,8192]{1,0:T(8,128)} %fusion.7.par_ref, bf16[128,512]{1,0:T(8,128)(2,1)} %get-tuple-element.33.bt_ref, ...), custom_call_target="tpu_custom_call" | custom-call | flops 805306368 | bytes 20971520 | tf_op jit(solution)/shard_map/own/pallas_call | solution.py:424
  64.0 17.6 %collective-permute-done.2.ex_ref = bf16[144,8192]{1,0:T(8,128)(2,1)} collective-permute-done((bf16[144,8192]{1,0:T(8,128)(2,1)}, bf16[144,8192]{1,0:T(8,128)(2,1)}, u32[]{:S(2)}, u32[]{:S(2)}) %collective-permute-start.2) | collective-permute-done | bytes 2359328 | tf_op jit(solution)/shard_map/ppermute | solution.py:367
  81.6 16.1 %extra.1 = (bf16[128,8192]{1,0:T(8,128)(2,1)}, f32[2,4,128,1024]{3,2,1,0:T(8,128)}, f32[2,4,136,1024]{3,2,1,0:T(8,128)}) custom-call(s32[1]{0:T(128)} %bitcast.odd_ref, bf16[144,8192]{1,0:T(8,128)(2,1)} %collective-permute-done.2.ex_ref, f32[8,8192]{1,0:T(8,128)} %fusion.7.par_ref, bf16[128,512]{1,0:T(8,128)(2,1)} %get-tuple-element.33.bt_ref, ...), custom_call_target="tpu_custom_call" | custom-call | flops 268435456 | bytes 20971520 | tf_op jit(solution)/shard_map/extra/pallas_call | solution.py:444
  97.7 4.4 %slice_bitcast_fusion = (f32[4,136,1024]{2,1,0:T(8,128)}, f32[4,136,1024]{2,1,0:T(8,128)S(1)}) fusion(f32[2,4,136,1024]{3,2,1,0:T(8,128)} %get-tuple-element.47), kind=kLoop, calls=%fused_computation | loop fusion | bytes 8912896 | tf_op jit(solution)/shard_map/squeeze | solution.py:497
  102.1 54.8 %all_to_all.20 = f32[4,136,1024]{2,1,0:T(8,128)S(1)} all-to-all(f32[4,136,1024]{2,1,0:T(8,128)S(1)} %get-tuple-element.71), channel_id=1, replica_groups=mesh['ctx'=8,'head'=4] {'head'}, dimensions={0} | all-to-all | bytes 4456448 | tf_op jit(solution)/shard_map/all_to_all | solution.py:467
  157.2 1.1 pad_maximum_fusion.2
  158.6 3.6 %all-to-all-start.1 = ((f32[4,136,1024]{2,1,0:T(8,128)}), f32[4,136,1024]{2,1,0:T(8,128)S(1)}, u32[]{:S(2)}, u32[]{:S(2)}) async-start(f32[4,136,1024]{2,1,0:T(8,128)} %get-tuple-element.49), calls=%async_computation.1 | async-start | bytes 4456448 | tf_op jit(solution)/shard_map/all_to_all | solution.py:467
  162.3 1.8 add_select_fusion.7
  164.1 0.8 pad_maximum_fusion.3
  164.9 1.5 collective-permute-start.4
  166.4 13.6 %collective-permute-done.4 = f32[136,1024]{1,0:T(8,128)} collective-permute-done((f32[136,1024]{1,0:T(8,128)}, f32[136,1024]{1,0:T(8,128)}, u32[]{:S(2)}, u32[]{:S(2)}) %collective-permute-start.4) | collective-permute-done | bytes 557088 | tf_op jit(solution)/shard_map/ppermute | solution.py:479
  180.0 0.8 slice_exponential_fusion.9
  180.8 1.1 add_select_fusion.6
  182.0 0.9 pad_maximum_fusion.4
  182.8 1.5 collective-permute-start.5
  184.3 12.7 %collective-permute-done.5 = f32[136,1024]{1,0:T(8,128)} collective-permute-done((f32[136,1024]{1,0:T(8,128)}, f32[136,1024]{1,0:T(8,128)}, u32[]{:S(2)}, u32[]{:S(2)}) %collective-permute-start.5) | collective-permute-done | bytes 557088 | tf_op jit(solution)/shard_map/ppermute | solution.py:479
  197.1 1.6 fusion.8
  198.9 1.6 pad_maximum_fusion
  200.5 13.4 %all-to-all-done.1 = f32[4,136,1024]{2,1,0:T(8,128)S(1)} async-done(((f32[4,136,1024]{2,1,0:T(8,128)}), f32[4,136,1024]{2,1,0:T(8,128)S(1)}, u32[]{:S(2)}, u32[]{:S(2)}) %all-to-all-start.1) | async-done | bytes 2228256 | tf_op jit(solution)/shard_map/all_to_all | solution.py:467
  214.2 4.5 %all-to-all-start.2 = ((f32[4,128,1024]{2,1,0:T(8,128)}), f32[4,128,1024]{2,1,0:T(8,128)}, u32[]{:S(2)}, u32[]{:S(2)}) async-start(f32[4,128,1024]{2,1,0:T(8,128)} %pad_maximum_fusion), calls=%async_computation.2 | async-start | bytes 4194304 | tf_op jit(solution)/shard_map/all_to_all | solution.py:467
  219.1 1.6 collective-permute-start.7
  220.7 13.5 %collective-permute-done.7 = f32[136,1024]{1,0:T(8,128)S(1)} collective-permute-done((f32[136,1024]{1,0:T(8,128)S(1)}, f32[136,1024]{1,0:T(8,128)S(1)}, u32[]{:S(2)}, u32[]{:S(2)}) %collective-permute-start.7) | collective-permute-done | bytes 557088 | tf_op jit(solution)/shard_map/ppermute | solution.py:479
  234.4 1.6 collective-permute-start.8
  236.0 12.8 %collective-permute-done.8 = f32[136,1024]{1,0:T(8,128)S(1)} collective-permute-done((f32[136,1024]{1,0:T(8,128)S(1)}, f32[136,1024]{1,0:T(8,128)S(1)}, u32[]{:S(2)}, u32[]{:S(2)}) %collective-permute-start.8) | collective-permute-done | bytes 557088 | tf_op jit(solution)/shard_map/ppermute | solution.py:479
  249.3 1.5 pad_maximum_fusion.1
  250.8 17.1 %all-to-all-done.2.ha_ref = f32[4,128,1024]{2,1,0:T(8,128)} async-done(((f32[4,128,1024]{2,1,0:T(8,128)}), f32[4,128,1024]{2,1,0:T(8,128)}, u32[]{:S(2)}, u32[]{:S(2)}) %all-to-all-start.2) | async-done | bytes 2097184 | tf_op jit(solution)/shard_map/all_to_all | solution.py:467
  267.9 3.8 %all-to-all-start.3 = ((f32[4,128,1024]{2,1,0:T(8,128)}), f32[4,128,1024]{2,1,0:T(8,128)S(1)}, u32[]{:S(2)}, u32[]{:S(2)}) async-start(f32[4,128,1024]{2,1,0:T(8,128)} %pad_maximum_fusion.1), calls=%async_computation.3 | async-start | bytes 4194304 | tf_op jit(solution)/shard_map/all_to_all | solution.py:467
  271.8 2.2 copy.17
  274.1 21.2 %diag.1.y_ref = f32[384,8192]{1,0:T(8,128)} custom-call(s32[1]{0:T(128)} %bitcast.odd_ref, bf16[384,8192]{1,0:T(8,128)(2,1)} %get-tuple-element.35.xc_ref, bf16[128,8192]{1,0:T(8,128)(2,1)} %get-tuple-element.40.xe_ref, f32[5,128,128]{2,1,0:T(8,128)} %get-tuple-element.41.s_ref, f32[16,384,8]{2,1,0:T(8,128)} %bitcast.138, ...), custom_call_target="tpu_custom_call" | custom-call | flops 2684354560 | bytes 20971520 | tf_op jit(solution)/shard_map/diag/pallas_call | solution.py:507
  295.3 24.5 %all-to-all-done.3.hb_ref = f32[4,128,1024]{2,1,0:T(8,128)S(1)} async-done(((f32[4,128,1024]{2,1,0:T(8,128)}), f32[4,128,1024]{2,1,0:T(8,128)S(1)}, u32[]{:S(2)}, u32[]{:S(2)}) %all-to-all-start.3) | async-done | bytes 2097184 | tf_op jit(solution)/shard_map/all_to_all | solution.py:467
  319.8 1.3 copy-done.2
  321.2 17.6 %gate.1 = bf16[384,8192]{1,0:T(8,128)(2,1)} custom-call(s32[1]{0:T(128)} %bitcast.odd_ref, f32[384,8192]{1,0:T(8,128)} %diag.1.y_ref, bf16[384,128]{1,0:T(8,128)(2,1)} %get-tuple-element.45.c_ref, f32[384,128]{1,0:T(8,128)} %get-tuple-element.46.ecs_ref, f32[4,128,1024]{2,1,0:T(8,128)} %all-to-all-done.2.ha_ref, f32[4,128,1024]{2,1,0:T(8,128)} %copy-done.2, ...), custom_call_target="tpu_custom_call" | custom-call | tf_op jit(solution)/shard_map/gate/pallas_call | solution.py:533
  (53 shorter events, 5.8 us)
Async XLA Ops:
  1.7 29.1 %collective-permute-start = (bf16[16,8448]{1,0:T(8,128)(2,1)S(1)}, bf16[16,8448]{1,0:T(8,128)(2,1)S(1)}, u32[]{:S(2)}, u32[]{:S(2)}) collective-permute-start(bf16[16,8448]{1,0:T(8,128)(2,1)S(1)} %pad_maximum_fusion.8), channel_id=1, source_target_pairs={{0,1},{1,2},{2,3},{3,4},{4,5},{5,6},{6,7},{7,8},{8,9},{9,10},{10,1... | collective-permute-start | bytes 811016 | tf_op jit(solution)/shard_map/ppermute | solution.py:361
  8.3 22.5 %collective-permute-start.1 = (bf16[144,384]{1,0:T(8,128)(2,1)S(1)}, bf16[144,384]{1,0:T(8,128)(2,1)S(1)}, u32[]{:S(2)}, u32[]{:S(2)}) collective-permute-start(bf16[144,384]{1,0:T(8,128)(2,1)S(1)} %pad_maximum_fusion.9), channel_id=1, source_target_pairs={{0,1},{2,3},{4,5},{6,7},{8,9},{10,11},{12,13},{14,15},{16,17},{18,... | collective-permute-start | bytes 331784 | tf_op jit(solution)/shard_map/ppermute | solution.py:364
  30.9 50.7 %collective-permute-start.2 = (bf16[144,8192]{1,0:T(8,128)(2,1)}, bf16[144,8192]{1,0:T(8,128)(2,1)}, u32[]{:S(2)}, u32[]{:S(2)}) collective-permute-start(bf16[144,8192]{1,0:T(8,128)(2,1)} %slice.151), channel_id=1, source_target_pairs={{0,1},{2,3},{4,5},{6,7},{8,9},{10,11},{12,13},{14,15},{16,17},{18,... | collective-permute-start | bytes 7077896 | tf_op jit(solution)/shard_map/ppermute | solution.py:367
  156.9 1.6 copy-start
  158.3 3.9 %collective-permute-start.3 = (f32[136,1024]{1,0:T(8,128)}, f32[136,1024]{1,0:T(8,128)S(1)}, u32[]{:S(2)}, u32[]{:S(2)}) collective-permute-start(f32[136,1024]{1,0:T(8,128)} %pad_maximum_fusion.2), channel_id=1, source_target_pairs={{0,4},{4,0},{8,12},{12,8},{16,20},{20,16},{24,28},{28,24},{1,5},{5... | collective-permute-start | bytes 1671176 | tf_op jit(solution)/shard_map/ppermute | solution.py:479
  158.6 55.3 %all-to-all-start.1 = ((f32[4,136,1024]{2,1,0:T(8,128)}), f32[4,136,1024]{2,1,0:T(8,128)S(1)}, u32[]{:S(2)}, u32[]{:S(2)}) async-start(f32[4,136,1024]{2,1,0:T(8,128)} %get-tuple-element.49), calls=%async_computation.1 | async-start | bytes 4456448 | tf_op jit(solution)/shard_map/all_to_all | solution.py:467
  164.9 15.1 %collective-permute-start.4 = (f32[136,1024]{1,0:T(8,128)}, f32[136,1024]{1,0:T(8,128)}, u32[]{:S(2)}, u32[]{:S(2)}) collective-permute-start(f32[136,1024]{1,0:T(8,128)} %pad_maximum_fusion.3), channel_id=1, source_target_pairs={{0,8},{4,12},{8,0},{12,4},{16,24},{20,28},{24,16},{28,20},{1,9},{5... | collective-permute-start | bytes 1671176 | tf_op jit(solution)/shard_map/ppermute | solution.py:479
  182.8 14.3 %collective-permute-start.5 = (f32[136,1024]{1,0:T(8,128)}, f32[136,1024]{1,0:T(8,128)}, u32[]{:S(2)}, u32[]{:S(2)}) collective-permute-start(f32[136,1024]{1,0:T(8,128)} %pad_maximum_fusion.4), channel_id=1, source_target_pairs={{0,16},{4,20},{8,24},{12,28},{16,0},{20,4},{24,8},{28,12},{1,17},{... | collective-permute-start | bytes 1671176 | tf_op jit(solution)/shard_map/ppermute | solution.py:479
  184.3 14.3 %copy-start.1 = (f32[4,136,1024]{2,1,0:T(8,128)S(1)}, f32[4,136,1024]{2,1,0:T(8,128)}, u32[]{:S(2)}) copy-start(f32[4,136,1024]{2,1,0:T(8,128)} %copy-done) | copy-start | bytes 6684676
  214.1 4.6 %collective-permute-start.6 = (f32[136,1024]{1,0:T(8,128)S(1)}, f32[136,1024]{1,0:T(8,128)S(1)}, u32[]{:S(2)}, u32[]{:S(2)}) collective-permute-start(f32[136,1024]{1,0:T(8,128)S(1)} %pad_maximum_fusion.5), channel_id=1, source_target_pairs={{0,4},{4,0},{8,12},{12,8},{16,20},{20,16},{24,28},{28,24},{1,5},{5... | collective-permute-start | bytes 1671176 | tf_op jit(solution)/shard_map/ppermute | solution.py:479
  214.2 53.7 %all-to-all-start.2 = ((f32[4,128,1024]{2,1,0:T(8,128)}), f32[4,128,1024]{2,1,0:T(8,128)}, u32[]{:S(2)}, u32[]{:S(2)}) async-start(f32[4,128,1024]{2,1,0:T(8,128)} %pad_maximum_fusion), calls=%async_computation.2 | async-start | bytes 4194304 | tf_op jit(solution)/shard_map/all_to_all | solution.py:467
  219.1 15.1 %collective-permute-start.7 = (f32[136,1024]{1,0:T(8,128)S(1)}, f32[136,1024]{1,0:T(8,128)S(1)}, u32[]{:S(2)}, u32[]{:S(2)}) collective-permute-start(f32[136,1024]{1,0:T(8,128)S(1)} %pad_maximum_fusion.6), channel_id=1, source_target_pairs={{0,8},{4,12},{8,0},{12,4},{16,24},{20,28},{24,16},{28,20},{1,9},{5... | collective-permute-start | bytes 1671176 | tf_op jit(solution)/shard_map/ppermute | solution.py:479
  234.4 14.4 %collective-permute-start.8 = (f32[136,1024]{1,0:T(8,128)S(1)}, f32[136,1024]{1,0:T(8,128)S(1)}, u32[]{:S(2)}, u32[]{:S(2)}) collective-permute-start(f32[136,1024]{1,0:T(8,128)S(1)} %pad_maximum_fusion.7), channel_id=1, source_target_pairs={{0,16},{4,20},{8,24},{12,28},{16,0},{20,4},{24,8},{28,12},{1,17},{... | collective-permute-start | bytes 1671176 | tf_op jit(solution)/shard_map/ppermute | solution.py:479
  250.8 20.9 %copy-start.3 = (f32[384,128]{1,0:T(8,128)S(1)}, f32[384,128]{1,0:T(8,128)}, u32[]{:S(2)}) copy-start(f32[384,128]{1,0:T(8,128)} %get-tuple-element.42) | copy-start | bytes 589828
  267.9 51.9 %all-to-all-start.3 = ((f32[4,128,1024]{2,1,0:T(8,128)}), f32[4,128,1024]{2,1,0:T(8,128)S(1)}, u32[]{:S(2)}, u32[]{:S(2)}) async-start(f32[4,128,1024]{2,1,0:T(8,128)} %pad_maximum_fusion.1), calls=%async_computation.3 | async-start | bytes 4194304 | tf_op jit(solution)/shard_map/all_to_all | solution.py:467
  319.8 1.3 copy-start.2
